TPU v7x, 512 devices: a whole 4x8x8 slice. The times are simulated.
512 devices in a mesh: tm: 256 (over z, x_lo, y, core), pts: 2 (over x_hi).
Axes of the slice: x: 4 (x_hi: 2, x_lo: 2; x = x_hi * 2 + x_lo), y: 8, z: 8, core: 2. Of those that a mesh axis runs over, the one named last changes fastest.
Arguments:
- features: bfloat16 [256, 64, 2048], P('tm', None, 'pts'), may hold values from -4.5 to 4.5
- positions: bfloat16 [256, 3, 2048], P('tm', None, 'pts'), may hold values from -6 to 6
- counts: int32 [256], replicated, may hold values from 512 to 2048, as said below
Outputs:
- velocity: float32 [256, 3, 2048], P('tm', None, 'pts')
Inputs may be any that keep to these rules, and one draw needn't show every extreme that they name: The usable points of a frame are its first counts entries.
All inputs are finite; a program needn't handle non-finite values.
Results may differ from a plain program's by a relative error of at most 0.0003.
Values may be sent and summed in bfloat16 or wider, within the bound.
A program may use at most 64 MiB of HBM per device.

v0:
```python
import math

import jax
import jax.numpy as jnp
from jax import lax
from jax.sharding import PartitionSpec as P

REACH = 3


score_scale = 0.25
neg_big = -1e30


def from_behind(block, axis, distance):
    devices = range(lax.axis_size(axis))
    route = [(i - distance, i) for i in devices if i - distance in devices]
    return lax.ppermute(block, axis, route)


def merged_2(value, axis, combine):
    everything = jax.tree.map(lambda part: lax.all_gather(part, axis), value)
    initial = jax.tree.map(lambda part: part[0], everything)

    def step(k, so_far):
        return combine(so_far, jax.tree.map(lambda part: part[k], everything))

    return lax.fori_loop(1, lax.axis_size(axis), step, initial)


def merge_stats(left_stats, right_stats):
    highest = jnp.maximum(left_stats[0], right_stats[0])
    scale_left = jnp.exp(left_stats[0] - highest)
    scale_right = jnp.exp(right_stats[0] - highest)
    summed = left_stats[1] * scale_left + right_stats[1] * scale_right
    weighted = left_stats[2] * jnp.expand_dims(scale_left, -2) + right_stats[2] * jnp.expand_dims(
        scale_right, -2
    )
    return (highest, summed, weighted)


def empty_stats(leading, col_count):
    return (
        jnp.full(leading + (col_count,), neg_big, jnp.float32),
        jnp.zeros(leading + (col_count,), jnp.float32),
        jnp.zeros(leading + (3, col_count), jnp.float32),
    )


def pair_block(src_feat, src_coords, src_usable, tgt_feat, tgt_coords, tgt_usable):
    row_count = src_feat.shape[1]
    col_count = tgt_feat.shape[1]
    stride = math.gcd(row_count, 512)

    def visit_block(col_stats, block_id):
        offset = block_id * stride
        feature_rows = lax.dynamic_slice_in_dim(src_feat, offset, stride, 1)
        coord_rows = lax.dynamic_slice_in_dim(src_coords, offset, stride, 1)
        usable_rows = lax.dynamic_slice_in_dim(src_usable, offset, stride, 0)
        scores = (
            lax.dot_general(
                feature_rows, tgt_feat, (((0,), (0,)), ((), ())), preferred_element_type=jnp.float32
            )
            * score_scale
        )
        row_out = ()
        masked = jnp.where(tgt_usable[None, :], scores, neg_big)
        highest = jnp.max(masked, axis=1)
        weights = jnp.where(tgt_usable[None, :], jnp.exp(masked - highest[:, None]), 0.0)
        weighted = lax.dot_general(
            tgt_coords,
            weights,
            (((1,), (1,)), ((), ())),
            precision=lax.Precision.HIGHEST,
            preferred_element_type=jnp.float32,
        )
        row_out = (highest, jnp.sum(weights, axis=1), weighted)
        masked = jnp.where(usable_rows[:, None], scores, neg_big)
        highest = jnp.max(masked, axis=0)
        weights = jnp.where(usable_rows[:, None], jnp.exp(masked - highest[None, :]), 0.0)
        fresh_stats = (
            highest,
            jnp.sum(weights, axis=0),
            jnp.dot(
                coord_rows,
                weights,
                precision=lax.Precision.HIGHEST,
                preferred_element_type=jnp.float32,
            ),
        )
        col_stats = merge_stats(col_stats, fresh_stats)
        return (col_stats, row_out)

    col_stats, row_parts = lax.scan(
        visit_block, empty_stats((), col_count), jnp.arange(row_count // stride, dtype=jnp.int32)
    )
    row_stats = None
    highest, summed, weighted = row_parts
    row_stats = (
        highest.reshape(row_count),
        summed.reshape(row_count),
        jnp.transpose(weighted, (1, 0, 2)).reshape(3, row_count),
    )
    return (row_stats, col_stats)


def per_device(features, positions, counts):
    frames = features.shape[0]
    half_pts = features.shape[2]
    pts_index = lax.axis_index("pts")
    frame_total = frames * lax.axis_size("tm")
    first_frame = lax.axis_index("tm") * frames
    distance_max = -(-REACH // frames)
    coords = positions.astype(jnp.float32)
    padded_counts = jnp.concatenate(
        [jnp.zeros((REACH,), jnp.int32), counts, jnp.zeros((REACH,), jnp.int32)]
    )
    own_points = pts_index * half_pts + jnp.arange(half_pts, dtype=jnp.int32)
    local_counts = lax.dynamic_slice_in_dim(padded_counts, first_frame + REACH, frames)
    own_usable = own_points[None, :] < local_counts[:, None]
    velocity = jnp.zeros((frames, 3, half_pts), jnp.float32)
    amounts = [
        min(frames, REACH - (distance - 1) * frames) for distance in range(1, distance_max + 1)
    ]
    pair_list = [(frame_id, offset) for frame_id in range(frames) for offset in range(1, REACH + 1)]
    pair_total = len(pair_list)
    ahead_feat = [features]
    ahead_pos = [positions]
    for distance in range(1, distance_max + 1):
        amount = amounts[distance - 1]
        arrived = from_behind((features, positions), "tm", -distance)
        ahead_feat.append(arrived[0])
        ahead_pos.append(arrived[1])
    ext_feat = jnp.concatenate(ahead_feat, 0)
    ext_pos = jnp.concatenate(ahead_pos, 0)
    ext_counts = lax.dynamic_slice_in_dim(padded_counts, first_frame + REACH, frames + REACH)
    row_init = empty_stats((pair_total,), half_pts)
    col_init = empty_stats((pair_total,), half_pts * lax.axis_size("pts"))
    start = jnp.int32(0)
    piece_feat = lax.all_gather(ext_feat[1:], "pts", axis=2, tiled=True)
    piece_pos = lax.all_gather(ext_pos[1:], "pts", axis=2, tiled=True)
    col_count = piece_feat.shape[2]
    col_index = jnp.arange(col_count, dtype=jnp.int32)
    row_carry = row_init
    col_carry = col_init
    for scan_pair_slot, (scan_frame_id, scan_offset) in enumerate(pair_list):
        target_id = scan_frame_id + scan_offset - 1
        tgt_usable = col_index < ext_counts[scan_frame_id + scan_offset]
        row_stats, col_stats = pair_block(
            features[scan_frame_id],
            coords[scan_frame_id],
            own_usable[scan_frame_id],
            piece_feat[target_id],
            piece_pos[target_id].astype(jnp.float32),
            tgt_usable,
        )
        previous = tuple((member[scan_pair_slot] for member in row_carry))
        merged = merge_stats(previous, row_stats)
        row_carry = tuple(
            (member.at[scan_pair_slot].set(value) for member, value in zip(row_carry, merged))
        )
        slot_id = jnp.int32(scan_pair_slot)
        col_carry = (
            lax.dynamic_update_slice(col_carry[0], col_stats[0][None, :], (slot_id, start)),
            lax.dynamic_update_slice(col_carry[1], col_stats[1][None, :], (slot_id, start)),
            lax.dynamic_update_slice(
                col_carry[2], col_stats[2][None, :, :], (slot_id, jnp.int32(0), start)
            ),
        )
    row_carry, col_carry = (row_carry, col_carry)
    row_peak, row_summed, row_acc = row_carry
    for pair_slot, (frame_id, offset) in enumerate(pair_list):
        live = first_frame + frame_id + offset < frame_total
        keep = own_usable[frame_id] & live
        safe = jnp.where(row_summed[pair_slot] > 0, row_summed[pair_slot], 1.0)
        forward = jnp.where(
            keep[None, :], row_acc[pair_slot] / safe[None, :] - coords[frame_id], 0.0
        )
        velocity = velocity.at[frame_id].add(forward / offset)
    col_peak, col_summed, col_acc = merged_2(col_carry, "pts", merge_stats)
    own_summed = lax.dynamic_slice_in_dim(col_summed, pts_index * half_pts, half_pts, 1)
    own_acc = lax.dynamic_slice_in_dim(col_acc, pts_index * half_pts, half_pts, 2)
    ext_usable = own_points[None, :] < ext_counts[:, None]
    ext_back = jnp.zeros((frames + REACH, 3, half_pts), jnp.float32)
    for pair_slot, (frame_id, offset) in enumerate(pair_list):
        target = frame_id + offset
        live = first_frame + target < frame_total
        keep = ext_usable[target] & live
        safe = jnp.where(own_summed[pair_slot] > 0, own_summed[pair_slot], 1.0)
        backward = jnp.where(
            keep[None, :],
            own_acc[pair_slot] / safe[None, :] - ext_pos[target].astype(jnp.float32),
            0.0,
        )
        ext_back = ext_back.at[target].add(-backward / offset)
    velocity = velocity + ext_back[:frames]
    for distance in range(1, distance_max + 1):
        amount = amounts[distance - 1]
        start_at = frames + (distance - 1) * frames
        arrived = from_behind(ext_back[start_at : start_at + amount], "tm", distance)
        velocity = velocity.at[:amount].add(arrived)
    global_index = first_frame + jnp.arange(frames, dtype=jnp.int32)
    term_count = jnp.minimum(REACH, frame_total - 1 - global_index) + jnp.minimum(
        REACH, global_index
    )
    return velocity / term_count.astype(jnp.float32)[:, None, None]


def solution(mesh):
    in_specs = (P("tm", None, "pts"), P("tm", None, "pts"), P())
    out_specs = P("tm", None, "pts")
    return jax.shard_map(
        per_device, mesh=mesh, in_specs=in_specs, out_specs=out_specs, check_vma=False
    )
```

profile of v0, /device:TPU:449, one launch (start us, length us, event | category | flops | bytes accessed | tf_op | source)
XLA Modules:
  0.0 179.8 jit_solution(18224592477940310923)
XLA Ops:
  2.6 6.0 %collective-permute-start.4 = (bf16[1,3,1024]{2,1,0:T(4,128)(2,1)}, bf16[1,3,1024]{2,1,0:T(4,128)(2,1)S(1)}, u32[]{:S(2)}, u32[]{:S(2)}) collective-permute-start(bf16[1,3,1024]{2,1,0:T(4,128)(2,1)} %param.50), channel_id=1, source_target_pairs={{4,0},{6,2},{8,4},{10,6},{12,8},{14,10},{16,12},{18,14},{20,16},{2... | collective-permute-start | bytes 18440 | tf_op jit(solution)/shard_map/ppermute | solution.py:18
  8.6 3.9 %collective-permute-start.5 = (bf16[1,3,1024]{2,1,0:T(4,128)(2,1)}, bf16[1,3,1024]{2,1,0:T(4,128)(2,1)S(1)}, u32[]{:S(2)}, u32[]{:S(2)}) collective-permute-start(bf16[1,3,1024]{2,1,0:T(4,128)(2,1)} %param.50), channel_id=1, source_target_pairs={{6,0},{8,2},{10,4},{12,6},{14,8},{16,10},{18,12},{20,14},{22,16},{... | collective-permute-start | bytes 18440 | tf_op jit(solution)/shard_map/ppermute | solution.py:18
  14.7 3.0 %collective-permute-start.1 = (bf16[1,64,1024]{2,1,0:T(8,128)(2,1)}, bf16[1,64,1024]{2,1,0:T(8,128)(2,1)S(1)}, u32[]{:S(2)}, u32[]{:S(2)}) collective-permute-start(bf16[1,64,1024]{2,1,0:T(8,128)(2,1)} %param.49), channel_id=1, source_target_pairs={{4,0},{6,2},{8,4},{10,6},{12,8},{14,10},{16,12},{18,14},{20,16},{2... | collective-permute-start | bytes 393224 | tf_op jit(solution)/shard_map/ppermute | solution.py:18
  25.4 4.9 %all_gather.37 = bf16[3,3,2048]{2,1,0:T(4,128)(2,1)S(1)} all-gather(bf16[3,3,1024]{2,1,0:T(4,128)(2,1)S(1)} %pad_maximum_fusion.1), channel_id=1, replica_groups=mesh['tm'=256,'pts'=2] {'pts'}, dimensions={2}, use_global_device_ids=true | all-gather | bytes 55296 | tf_op jit(solution)/shard_map/all_gather | solution.py:141
  32.9 12.9 %all_gather.36 = bf16[3,64,2048]{2,1,0:T(8,128)(2,1)S(1)} all-gather(bf16[3,64,1024]{2,1,0:T(8,128)(2,1)S(1)} %pad_maximum_fusion), channel_id=1, replica_groups=mesh['tm'=256,'pts'=2] {'pts'}, dimensions={2}, use_global_device_ids=true | all-gather | bytes 1179648 | tf_op jit(solution)/shard_map/all_gather | solution.py:140
  45.8 33.2 %while.91 = (s32[]{:T(128)}, f32[2048]{0:T(1024)S(1)}, f32[2048]{0:T(1024)S(1)}, f32[3,2048]{1,0:T(4,128)S(1)}, f32[2,512]{1,0:T(2,128)S(1)}, /*index=5*/f32[2,5...) while((s32[]{:T(128)}, f32[2048]{0:T(1024)S(1)}, ...), condition=%wide.region_11.12_spmd.clone, body=%wide.region_6.11_spmd.clone.sunk | while | flops 232821760 | bytes 34130720 | solution.py:94
  49.9 4.5 %fusion.156 = f32[2,3,512]{2,1,0:T(4,128)S(1)} fusion(f32[2,3,512]{2,1,0:T(4,128)S(1)} %get-tuple-element.1189, s32[]{:T(128)} %get-tuple-element.1183, f32[3,2048]{1,0:T(4,128)S(1)} %get-tuple-element.1213, f32[512,2048]{1,0:T(8,128)S(1)} %get-tuple-element.1079, f32[512]{0:T(512)S(1)} %get-tuple-element.1080, ...), kind=kOutput, calls=%fused_computation.64.clone.1 | convolution fusion | flops 41943040 | bytes 4239364 | tf_op jit(solution)/shard_map/while/body/eval_jaxpr/dot_general | solution.py:70
  54.4 2.8 %fusion.153 = (f32[512]{0:T(512)S(1)}, f32[2048]{0:T(1024)S(1)}) fusion(f32[512,2048]{1,0:T(8,128)S(1)} %get-tuple-element.1079, f32[512]{0:T(512)S(1)} %get-tuple-element.1080, pred[2048]{0:T(1024)(128)(4,1)S(1)} %iota_compare_fusion.7, f32[2048]{0:T(1024)S(1)} %get-tuple-element.1081, pred[512]{0:T(512)(128)(4,1)S(1)} %dynamic_slice.145), kind=kLoop, calls=%fused_computation.50.clone.1 | loop fusion | flops 9434624 | bytes 4217344 | tf_op jit(solution)/shard_map/while/body/eval_jaxpr/reduce_sum | solution.py:77
  57.2 5.2 %fusion.155 = f32[3,2048]{1,0:T(4,128)S(1)} fusion(f32[512,2048]{1,0:T(8,128)} %copy-done, f32[2048]{0:T(1024)S(1)} %get-tuple-element.1081, pred[512]{0:T(512)(128)(4,1)S(1)} %dynamic_slice.145, f32[3,2048]{1,0:T(4,128)S(1)} %get-tuple-element.1186, f32[2048]{0:T(1024)S(1)} %get-tuple-element.1085, f32[2048]{0:T(1024)S(1)} %get-tuple-element.1086, ...), kind=kOutput, calls=%fused_computation.52.clone.1 | convolution fusion | flops 41967616 | bytes 4284933 | tf_op jit(solution)/shard_map/while/body/eval_jaxpr/dot_general | solution.py:84
  66.5 4.5 %fusion.156 = f32[2,3,512]{2,1,0:T(4,128)S(1)} fusion(f32[2,3,512]{2,1,0:T(4,128)S(1)} %get-tuple-element.1189, s32[]{:T(128)} %get-tuple-element.1183, f32[3,2048]{1,0:T(4,128)S(1)} %get-tuple-element.1213, f32[512,2048]{1,0:T(8,128)S(1)} %get-tuple-element.1079, f32[512]{0:T(512)S(1)} %get-tuple-element.1080, ...), kind=kOutput, calls=%fused_computation.64.clone.1 | convolution fusion | flops 41943040 | bytes 4239364 | tf_op jit(solution)/shard_map/while/body/eval_jaxpr/dot_general | solution.py:70
  71.0 2.8 %fusion.153 = (f32[512]{0:T(512)S(1)}, f32[2048]{0:T(1024)S(1)}) fusion(f32[512,2048]{1,0:T(8,128)S(1)} %get-tuple-element.1079, f32[512]{0:T(512)S(1)} %get-tuple-element.1080, pred[2048]{0:T(1024)(128)(4,1)S(1)} %iota_compare_fusion.7, f32[2048]{0:T(1024)S(1)} %get-tuple-element.1081, pred[512]{0:T(512)(128)(4,1)S(1)} %dynamic_slice.145), kind=kLoop, calls=%fused_computation.50.clone.1 | loop fusion | flops 9434624 | bytes 4217344 | tf_op jit(solution)/shard_map/while/body/eval_jaxpr/reduce_sum | solution.py:77
  73.8 5.2 %fusion.155 = f32[3,2048]{1,0:T(4,128)S(1)} fusion(f32[512,2048]{1,0:T(8,128)} %copy-done, f32[2048]{0:T(1024)S(1)} %get-tuple-element.1081, pred[512]{0:T(512)(128)(4,1)S(1)} %dynamic_slice.145, f32[3,2048]{1,0:T(4,128)S(1)} %get-tuple-element.1186, f32[2048]{0:T(1024)S(1)} %get-tuple-element.1085, f32[2048]{0:T(1024)S(1)} %get-tuple-element.1086, ...), kind=kOutput, calls=%fused_computation.52.clone.1 | convolution fusion | flops 41967616 | bytes 4284933 | tf_op jit(solution)/shard_map/while/body/eval_jaxpr/dot_general | solution.py:84
  79.1 33.4 %while.90 = (s32[]{:T(128)}, f32[2048]{0:T(1024)S(1)}, f32[2048]{0:T(1024)S(1)}, f32[3,2048]{1,0:T(4,128)S(1)}, f32[2,512]{1,0:T(2,128)S(1)}, /*index=5*/f32[2,5...) while((s32[]{:T(128)}, f32[2048]{0:T(1024)S(1)}, ...), condition=%wide.region_5.6_spmd.clone, body=%wide.region_0.5_spmd.clone.sunk | while | flops 232821760 | bytes 34130720 | solution.py:94
  83.4 4.5 %fusion.149 = f32[2,3,512]{2,1,0:T(4,128)S(1)} fusion(f32[2,3,512]{2,1,0:T(4,128)S(1)} %get-tuple-element.1135, s32[]{:T(128)} %get-tuple-element.1129, f32[3,2048]{1,0:T(4,128)S(1)} %get-tuple-element.1159, f32[512,2048]{1,0:T(8,128)S(1)} %get-tuple-element.1056, f32[512]{0:T(512)S(1)} %get-tuple-element.1057, ...), kind=kOutput, calls=%fused_computation.24.clone.1 | convolution fusion | flops 41943040 | bytes 4239364 | tf_op jit(solution)/shard_map/while/body/eval_jaxpr/dot_general | solution.py:70
  87.8 2.8 %fusion.146 = (f32[512]{0:T(512)S(1)}, f32[2048]{0:T(1024)S(1)}) fusion(f32[512,2048]{1,0:T(8,128)S(1)} %get-tuple-element.1056, f32[512]{0:T(512)S(1)} %get-tuple-element.1057, pred[2048]{0:T(1024)(128)(4,1)S(1)} %iota_compare_fusion.6, f32[2048]{0:T(1024)S(1)} %get-tuple-element.1058, pred[512]{0:T(512)(128)(4,1)S(1)} %dynamic_slice.141), kind=kLoop, calls=%fused_computation.10.clone.1 | loop fusion | flops 9434624 | bytes 4217344 | tf_op jit(solution)/shard_map/while/body/eval_jaxpr/reduce_sum | solution.py:77
  90.6 5.2 %fusion.148 = f32[3,2048]{1,0:T(4,128)S(1)} fusion(f32[512,2048]{1,0:T(8,128)} %copy-done.1, f32[2048]{0:T(1024)S(1)} %get-tuple-element.1058, pred[512]{0:T(512)(128)(4,1)S(1)} %dynamic_slice.141, f32[3,2048]{1,0:T(4,128)S(1)} %get-tuple-element.1132, f32[2048]{0:T(1024)S(1)} %get-tuple-element.1062, f32[2048]{0:T(1024)S(1)} %get-tuple-element.1063, ...), kind=kOutput, calls=%fused_computation.12.clone.1 | convolution fusion | flops 41967616 | bytes 4284933 | tf_op jit(solution)/shard_map/while/body/eval_jaxpr/dot_general | solution.py:84
  100.0 4.5 %fusion.149 = f32[2,3,512]{2,1,0:T(4,128)S(1)} fusion(f32[2,3,512]{2,1,0:T(4,128)S(1)} %get-tuple-element.1135, s32[]{:T(128)} %get-tuple-element.1129, f32[3,2048]{1,0:T(4,128)S(1)} %get-tuple-element.1159, f32[512,2048]{1,0:T(8,128)S(1)} %get-tuple-element.1056, f32[512]{0:T(512)S(1)} %get-tuple-element.1057, ...), kind=kOutput, calls=%fused_computation.24.clone.1 | convolution fusion | flops 41943040 | bytes 4239364 | tf_op jit(solution)/shard_map/while/body/eval_jaxpr/dot_general | solution.py:70
  104.5 2.8 %fusion.146 = (f32[512]{0:T(512)S(1)}, f32[2048]{0:T(1024)S(1)}) fusion(f32[512,2048]{1,0:T(8,128)S(1)} %get-tuple-element.1056, f32[512]{0:T(512)S(1)} %get-tuple-element.1057, pred[2048]{0:T(1024)(128)(4,1)S(1)} %iota_compare_fusion.6, f32[2048]{0:T(1024)S(1)} %get-tuple-element.1058, pred[512]{0:T(512)(128)(4,1)S(1)} %dynamic_slice.141), kind=kLoop, calls=%fused_computation.10.clone.1 | loop fusion | flops 9434624 | bytes 4217344 | tf_op jit(solution)/shard_map/while/body/eval_jaxpr/reduce_sum | solution.py:77
  107.3 5.2 %fusion.148 = f32[3,2048]{1,0:T(4,128)S(1)} fusion(f32[512,2048]{1,0:T(8,128)} %copy-done.1, f32[2048]{0:T(1024)S(1)} %get-tuple-element.1058, pred[512]{0:T(512)(128)(4,1)S(1)} %dynamic_slice.141, f32[3,2048]{1,0:T(4,128)S(1)} %get-tuple-element.1132, f32[2048]{0:T(1024)S(1)} %get-tuple-element.1062, f32[2048]{0:T(1024)S(1)} %get-tuple-element.1063, ...), kind=kOutput, calls=%fused_computation.12.clone.1 | convolution fusion | flops 41967616 | bytes 4284933 | tf_op jit(solution)/shard_map/while/body/eval_jaxpr/dot_general | solution.py:84
  112.6 33.2 %while.92 = (s32[]{:T(128)}, f32[2048]{0:T(1024)S(1)}, f32[2048]{0:T(1024)S(1)}, f32[3,2048]{1,0:T(4,128)S(1)}, f32[2,512]{1,0:T(2,128)S(1)}, /*index=5*/f32[2,5...) while((s32[]{:T(128)}, f32[2048]{0:T(1024)S(1)}, ...), condition=%wide.region_17.18_spmd.clone, body=%wide.region_12.0_spmd.clone.sunk | while | flops 232821760 | bytes 34130720 | solution.py:94
  116.8 4.5 %fusion.163 = f32[2,3,512]{2,1,0:T(4,128)S(1)} fusion(f32[2,3,512]{2,1,0:T(4,128)S(1)} %get-tuple-element.1243, s32[]{:T(128)} %get-tuple-element.1237, f32[3,2048]{1,0:T(4,128)S(1)} %get-tuple-element.1267, f32[512,2048]{1,0:T(8,128)S(1)} %get-tuple-element.1102, f32[512]{0:T(512)S(1)} %get-tuple-element.1103, ...), kind=kOutput, calls=%fused_computation.104.clone.1 | convolution fusion | flops 41943040 | bytes 4239364 | tf_op jit(solution)/shard_map/while/body/eval_jaxpr/dot_general | solution.py:70
  121.3 2.8 %fusion.160 = (f32[512]{0:T(512)S(1)}, f32[2048]{0:T(1024)S(1)}) fusion(f32[512,2048]{1,0:T(8,128)S(1)} %get-tuple-element.1102, f32[512]{0:T(512)S(1)} %get-tuple-element.1103, pred[2048]{0:T(1024)(128)(4,1)S(1)} %iota_compare_fusion.8, f32[2048]{0:T(1024)S(1)} %get-tuple-element.1104, pred[512]{0:T(512)(128)(4,1)S(1)} %dynamic_slice.149), kind=kLoop, calls=%fused_computation.90.clone.1 | loop fusion | flops 9434624 | bytes 4217344 | tf_op jit(solution)/shard_map/while/body/eval_jaxpr/reduce_sum | solution.py:77
  124.1 5.2 %fusion.162 = f32[3,2048]{1,0:T(4,128)S(1)} fusion(f32[512,2048]{1,0:T(8,128)} %copy-done.2, f32[2048]{0:T(1024)S(1)} %get-tuple-element.1104, pred[512]{0:T(512)(128)(4,1)S(1)} %dynamic_slice.149, f32[3,2048]{1,0:T(4,128)S(1)} %get-tuple-element.1240, f32[2048]{0:T(1024)S(1)} %get-tuple-element.1108, f32[2048]{0:T(1024)S(1)} %get-tuple-element.1109, ...), kind=kOutput, calls=%fused_computation.92.clone.1 | convolution fusion | flops 41967616 | bytes 4284933 | tf_op jit(solution)/shard_map/while/body/eval_jaxpr/dot_general | solution.py:84
  133.3 4.5 %fusion.163 = f32[2,3,512]{2,1,0:T(4,128)S(1)} fusion(f32[2,3,512]{2,1,0:T(4,128)S(1)} %get-tuple-element.1243, s32[]{:T(128)} %get-tuple-element.1237, f32[3,2048]{1,0:T(4,128)S(1)} %get-tuple-element.1267, f32[512,2048]{1,0:T(8,128)S(1)} %get-tuple-element.1102, f32[512]{0:T(512)S(1)} %get-tuple-element.1103, ...), kind=kOutput, calls=%fused_computation.104.clone.1 | convolution fusion | flops 41943040 | bytes 4239364 | tf_op jit(solution)/shard_map/while/body/eval_jaxpr/dot_general | solution.py:70
  137.8 2.8 %fusion.160 = (f32[512]{0:T(512)S(1)}, f32[2048]{0:T(1024)S(1)}) fusion(f32[512,2048]{1,0:T(8,128)S(1)} %get-tuple-element.1102, f32[512]{0:T(512)S(1)} %get-tuple-element.1103, pred[2048]{0:T(1024)(128)(4,1)S(1)} %iota_compare_fusion.8, f32[2048]{0:T(1024)S(1)} %get-tuple-element.1104, pred[512]{0:T(512)(128)(4,1)S(1)} %dynamic_slice.149), kind=kLoop, calls=%fused_computation.90.clone.1 | loop fusion | flops 9434624 | bytes 4217344 | tf_op jit(solution)/shard_map/while/body/eval_jaxpr/reduce_sum | solution.py:77
  140.6 5.2 %fusion.162 = f32[3,2048]{1,0:T(4,128)S(1)} fusion(f32[512,2048]{1,0:T(8,128)} %copy-done.2, f32[2048]{0:T(1024)S(1)} %get-tuple-element.1104, pred[512]{0:T(512)(128)(4,1)S(1)} %dynamic_slice.149, f32[3,2048]{1,0:T(4,128)S(1)} %get-tuple-element.1240, f32[2048]{0:T(1024)S(1)} %get-tuple-element.1108, f32[2048]{0:T(1024)S(1)} %get-tuple-element.1109, ...), kind=kOutput, calls=%fused_computation.92.clone.1 | convolution fusion | flops 41967616 | bytes 4284933 | tf_op jit(solution)/shard_map/while/body/eval_jaxpr/dot_general | solution.py:84
  146.1 4.9 %all_gather.45 = f32[2,3,2048]{2,1,0:T(4,128)S(1)} all-gather(f32[1,3,2048]{2,1,0:T(4,128)S(1)} %dynamic_update_slice.67), channel_id=1, replica_groups=mesh['tm'=256,'pts'=2] {'pts'}, dimensions={0}, use_global_device_ids=true | all-gather | bytes 73728 | tf_op jit(solution)/shard_map/all_gather | solution.py:22
  151.4 4.9 %all_gather.49 = f32[2,3,2048]{2,1,0:T(4,128)S(1)} all-gather(f32[1,3,2048]{2,1,0:T(4,128)S(1)} %dynamic_update_slice.70), channel_id=1, replica_groups=mesh['tm'=256,'pts'=2] {'pts'}, dimensions={0}, use_global_device_ids=true | all-gather | bytes 73728 | tf_op jit(solution)/shard_map/all_gather | solution.py:22
  156.4 5.6 %all_gather.41 = f32[2,3,3,2048]{3,2,1,0:T(4,128)S(1)} all-gather(f32[1,3,3,2048]{3,2,1,0:T(4,128)S(1)} %bitcast_dynamic-update-slice_fusion), channel_id=1, replica_groups=mesh['tm'=256,'pts'=2] {'pts'}, dimensions={0}, use_global_device_ids=true | all-gather | bytes 221184 | tf_op jit(solution)/shard_map/all_gather | solution.py:22
  162.2 5.8 %collective-permute-start.6 = (f32[1,3,1024]{2,1,0:T(4,128)S(1)}, f32[1,3,1024]{2,1,0:T(4,128)S(1)}, u32[]{:S(2)}, u32[]{:S(2)}) collective-permute-start(f32[1,3,1024]{2,1,0:T(4,128)S(1)} %get-tuple-element.773), channel_id=1, source_target_pairs={{0,2},{2,4},{4,6},{6,8},{8,10},{10,12},{12,14},{14,16},{16,18},{18... | collective-permute-start | bytes 36872 | tf_op jit(solution)/shard_map/ppermute | solution.py:18
  168.0 3.1 %collective-permute-start.7 = (f32[1,3,1024]{2,1,0:T(4,128)S(1)}, f32[1,3,1024]{2,1,0:T(4,128)S(1)}, u32[]{:S(2)}, u32[]{:S(2)}) collective-permute-start(f32[1,3,1024]{2,1,0:T(4,128)S(1)} %get-tuple-element.774), channel_id=1, source_target_pairs={{0,4},{2,6},{4,8},{6,10},{8,12},{10,14},{12,16},{14,18},{16,20},{1... | collective-permute-start | bytes 36872 | tf_op jit(solution)/shard_map/ppermute | solution.py:18
  175.5 3.7 %collective-permute-done.8 = f32[1,3,1024]{2,1,0:T(4,128)S(1)} collective-permute-done((f32[1,3,1024]{2,1,0:T(4,128)S(1)}, f32[1,3,1024]{2,1,0:T(4,128)S(1)}, u32[]{:S(2)}, u32[]{:S(2)}) %collective-permute-start.8) | collective-permute-done | bytes 12320 | tf_op jit(solution)/shard_map/ppermute | solution.py:18
  (131 shorter events, 41.5 us)
Async XLA Ops:
  0.0 22.6 %collective-permute-start.3 = (bf16[1,3,1024]{2,1,0:T(4,128)(2,1)}, bf16[1,3,1024]{2,1,0:T(4,128)(2,1)S(1)}, u32[]{:S(2)}, u32[]{:S(2)}) collective-permute-start(bf16[1,3,1024]{2,1,0:T(4,128)(2,1)} %param.50), channel_id=1, source_target_pairs={{2,0},{4,2},{6,4},{8,6},{10,8},{12,10},{14,12},{16,14},{18,16},{20... | collective-permute-start | bytes 18440 | tf_op jit(solution)/shard_map/ppermute | solution.py:18
  2.6 22.8 %collective-permute-start.4 = (bf16[1,3,1024]{2,1,0:T(4,128)(2,1)}, bf16[1,3,1024]{2,1,0:T(4,128)(2,1)S(1)}, u32[]{:S(2)}, u32[]{:S(2)}) collective-permute-start(bf16[1,3,1024]{2,1,0:T(4,128)(2,1)} %param.50), channel_id=1, source_target_pairs={{4,0},{6,2},{8,4},{10,6},{12,8},{14,10},{16,12},{18,14},{20,16},{2... | collective-permute-start | bytes 18440 | tf_op jit(solution)/shard_map/ppermute | solution.py:18
  8.6 16.8 %collective-permute-start.5 = (bf16[1,3,1024]{2,1,0:T(4,128)(2,1)}, bf16[1,3,1024]{2,1,0:T(4,128)(2,1)S(1)}, u32[]{:S(2)}, u32[]{:S(2)}) collective-permute-start(bf16[1,3,1024]{2,1,0:T(4,128)(2,1)} %param.50), channel_id=1, source_target_pairs={{6,0},{8,2},{10,4},{12,6},{14,8},{16,10},{18,12},{20,14},{22,16},{... | collective-permute-start | bytes 18440 | tf_op jit(solution)/shard_map/ppermute | solution.py:18
  12.5 17.7 %collective-permute-start = (bf16[1,64,1024]{2,1,0:T(8,128)(2,1)}, bf16[1,64,1024]{2,1,0:T(8,128)(2,1)S(1)}, u32[]{:S(2)}, u32[]{:S(2)}) collective-permute-start(bf16[1,64,1024]{2,1,0:T(8,128)(2,1)} %param.49), channel_id=1, source_target_pairs={{2,0},{4,2},{6,4},{8,6},{10,8},{12,10},{14,12},{16,14},{18,16},{20... | collective-permute-start | bytes 393224 | tf_op jit(solution)/shard_map/ppermute | solution.py:18
  14.7 15.6 %collective-permute-start.1 = (bf16[1,64,1024]{2,1,0:T(8,128)(2,1)}, bf16[1,64,1024]{2,1,0:T(8,128)(2,1)S(1)}, u32[]{:S(2)}, u32[]{:S(2)}) collective-permute-start(bf16[1,64,1024]{2,1,0:T(8,128)(2,1)} %param.49), channel_id=1, source_target_pairs={{4,0},{6,2},{8,4},{10,6},{12,8},{14,10},{16,12},{18,14},{20,16},{2... | collective-permute-start | bytes 393224 | tf_op jit(solution)/shard_map/ppermute | solution.py:18
  22.6 10.2 %collective-permute-start.2 = (bf16[1,64,1024]{2,1,0:T(8,128)(2,1)}, bf16[1,64,1024]{2,1,0:T(8,128)(2,1)S(1)}, u32[]{:S(2)}, u32[]{:S(2)}) collective-permute-start(bf16[1,64,1024]{2,1,0:T(8,128)(2,1)} %param.49), channel_id=1, source_target_pairs={{6,0},{8,2},{10,4},{12,6},{14,8},{16,10},{18,12},{20,14},{22,16},{... | collective-permute-start | bytes 393224 | tf_op jit(solution)/shard_map/ppermute | solution.py:18
  49.9 7.2 %copy-start = (f32[512,2048]{1,0:T(8,128)}, f32[512,2048]{1,0:T(8,128)S(1)}, u32[]{:S(2)}) copy-start(f32[512,2048]{1,0:T(8,128)S(1)} %get-tuple-element.1079) | copy-start | bytes 12582916 | tf_op jit(solution)/shard_map/while
  66.5 7.2 %copy-start = (f32[512,2048]{1,0:T(8,128)}, f32[512,2048]{1,0:T(8,128)S(1)}, u32[]{:S(2)}) copy-start(f32[512,2048]{1,0:T(8,128)S(1)} %get-tuple-element.1079) | copy-start | bytes 12582916 | tf_op jit(solution)/shard_map/while
  83.4 7.2 %copy-start.1 = (f32[512,2048]{1,0:T(8,128)}, f32[512,2048]{1,0:T(8,128)S(1)}, u32[]{:S(2)}) copy-start(f32[512,2048]{1,0:T(8,128)S(1)} %get-tuple-element.1056) | copy-start | bytes 12582916 | tf_op jit(solution)/shard_map/while
  100.0 7.2 %copy-start.1 = (f32[512,2048]{1,0:T(8,128)}, f32[512,2048]{1,0:T(8,128)S(1)}, u32[]{:S(2)}) copy-start(f32[512,2048]{1,0:T(8,128)S(1)} %get-tuple-element.1056) | copy-start | bytes 12582916 | tf_op jit(solution)/shard_map/while
  112.6 66.6 %copy-start.3 = (bf16[1,3,1024]{2,1,0:T(4,128)(2,1)S(1)}, bf16[1,3,1024]{2,1,0:T(4,128)(2,1)}, u32[]{:S(2)}) copy-start(bf16[1,3,1024]{2,1,0:T(4,128)(2,1)} %param.50) | copy-start | bytes 18436
  116.8 7.2 %copy-start.2 = (f32[512,2048]{1,0:T(8,128)}, f32[512,2048]{1,0:T(8,128)S(1)}, u32[]{:S(2)}) copy-start(f32[512,2048]{1,0:T(8,128)S(1)} %get-tuple-element.1102) | copy-start | bytes 12582916 | tf_op jit(solution)/shard_map/while
  133.3 7.2 %copy-start.2 = (f32[512,2048]{1,0:T(8,128)}, f32[512,2048]{1,0:T(8,128)S(1)}, u32[]{:S(2)}) copy-start(f32[512,2048]{1,0:T(8,128)S(1)} %get-tuple-element.1102) | copy-start | bytes 12582916 | tf_op jit(solution)/shard_map/while
  162.2 11.5 %collective-permute-start.6 = (f32[1,3,1024]{2,1,0:T(4,128)S(1)}, f32[1,3,1024]{2,1,0:T(4,128)S(1)}, u32[]{:S(2)}, u32[]{:S(2)}) collective-permute-start(f32[1,3,1024]{2,1,0:T(4,128)S(1)} %get-tuple-element.773), channel_id=1, source_target_pairs={{0,2},{2,4},{4,6},{6,8},{8,10},{10,12},{12,14},{14,16},{16,18},{18... | collective-permute-start | bytes 36872 | tf_op jit(solution)/shard_map/ppermute | solution.py:18
  168.0 7.5 %collective-permute-start.7 = (f32[1,3,1024]{2,1,0:T(4,128)S(1)}, f32[1,3,1024]{2,1,0:T(4,128)S(1)}, u32[]{:S(2)}, u32[]{:S(2)}) collective-permute-start(f32[1,3,1024]{2,1,0:T(4,128)S(1)} %get-tuple-element.774), channel_id=1, source_target_pairs={{0,4},{2,6},{4,8},{6,10},{8,12},{10,14},{12,16},{14,18},{16,20},{1... | collective-permute-start | bytes 36872 | tf_op jit(solution)/shard_map/ppermute | solution.py:18
  171.1 8.1 %collective-permute-start.8 = (f32[1,3,1024]{2,1,0:T(4,128)S(1)}, f32[1,3,1024]{2,1,0:T(4,128)S(1)}, u32[]{:S(2)}, u32[]{:S(2)}) collective-permute-start(f32[1,3,1024]{2,1,0:T(4,128)S(1)} %get-tuple-element.775), channel_id=1, source_target_pairs={{0,6},{2,8},{4,10},{6,12},{8,14},{10,16},{12,18},{14,20},{16,22},{... | collective-permute-start | bytes 36872 | tf_op jit(solution)/shard_map/ppermute | solution.py:18
where the time goes:
time: 181 us; the launch traced here: 180 us
  matrix products  70 us (39%)
  blocking collectives  33.3 us (18%)
  starting transfers between devices  31.8 us (18%)
  other arithmetic  24.1 us (13%)
  waiting for transfers between devices  7.94 us (4%)
  local copies, waits for them, and re-layouts  7.43 us (4%)
  loops' own time  4.86 us (3%)
    ppermute x9, starting transfers between devices, from_behind(): return lax.ppermute(block, axis, route)  31.8 us
    dot_general x6, matrix products, visit_block(): jnp.dot(coord_rows, weights, precision=lax.Precision.HIGHEST, preferred_e...  30.9 us
    dot_general x6, matrix products, visit_block(): lax.dot_general(tgt_coords, weights, (((1,), (1,)), ((), ())), precision=...  26.8 us
    reduce_sum x6, other arithmetic, visit_block(): row_out = (highest, jnp.sum(weights, axis=1), weighted)  16.5 us
    all_gather x3, blocking collectives, merged_2(): everything = jax.tree.map(lambda part: lax.all_gather(part, axis), value)  15.5 us
    all_gather x1, blocking collectives, per_device(): piece_feat = lax.all_gather(ext_feat[1:], 'pts', axis=2, tiled=True)  12.9 us
    dot_general x6, matrix products, visit_block(): lax.dot_general(feature_rows, tgt_feat, (((0,), (0,)), ((), ())), preferr...  12.2 us
    ppermute x9, waiting for transfers between devices, from_behind(): return lax.ppermute(block, axis, route)  7.94 us
  transfers between devices with their start and end apart: 9, of which 3 were waited for; matrix products, arithmetic and copies ran while one was open for 3% of the time, Pallas kernels for 0%

commit v1 on v0

v1 whole, which is shorter than its diff:
```python
import functools

import jax
import jax.numpy as jnp
from jax import lax
from jax.experimental import pallas as pl
from jax.experimental.pallas import tpu as pltpu
from jax.sharding import PartitionSpec as P

REACH = 3
CHANNELS = 64
HALF = 1024
PACK = HALF // 2
POS_ROWS = 32
MSG = PACK + POS_ROWS
SCORE_SCALE = 0.25
LOG2E = 1.4426950408889634
DEN_LOW = 2.0**-90
DEN_HIGH = 2.0**100
MESH = pl.DeviceIdType.MESH
f32 = jnp.float32
bf16 = jnp.bfloat16

OFFSETS = (1, 2, -1, -2, 3, -3)
FRAME_SLOTS = len(OFFSETS)
SLOTS = 2 * FRAME_SLOTS
XM = SLOTS


def wrapped(frame, total):
    return lax.rem(frame + total, total)


def pack_message(feat, pos, usable):
    kept = jnp.where(usable, feat.astype(f32), 0.0)
    rows = jnp.concatenate([kept[:, :PACK], kept[:, PACK:]], axis=0).T
    flag = usable.astype(f32)
    quad = jnp.concatenate([jnp.where(usable, pos.astype(f32), 0.0), flag], axis=0)
    tail = jnp.concatenate([quad[:, q * 128 : (q + 1) * 128] for q in range(HALF // 128)], axis=0)
    return rows.astype(bf16), tail.astype(bf16)


def position_rows(tail):
    tail = tail.astype(f32)
    pieces = []
    for j in range(POS_ROWS // 8):
        block = tail[j * 8 : j * 8 + 8]
        pieces.append(block)
        pieces.append(jnp.concatenate([block[4:], block[:4]], axis=0))
    return jnp.concatenate(pieces, axis=1).astype(bf16)


def gather_and_match(
    total, cnt_ref, feat_ref, pos_ref, out_ref, kept_ref, own, xm, keys, weights, acc, send_sem, recv_sem, keep_sem
):
    t = lax.axis_index("tm")
    p = lax.axis_index("pts")
    sigma = 1 - 2 * lax.rem(t, 2)
    sibling = wrapped(t + sigma, total)
    across = wrapped(t - sigma, total)
    near = wrapped(t - 2 * sigma, total)
    far = wrapped(t + 2 * sigma, total)
    partners = [(t, 1 - p), (sibling, p), (across, p), (near, p), (far, p)]

    barrier = pltpu.get_barrier_semaphore()
    for partner in partners:
        pl.semaphore_signal(barrier, inc=1, device_id=partner, device_id_type=MESH)

    point = lax.broadcasted_iota(jnp.int32, (1, HALF), 1) + p * HALF
    usable = point < cnt_ref[t]
    rows, tail = pack_message(feat_ref[0], pos_ref[0], usable)
    own[:PACK] = rows
    own[PACK:] = tail

    pl.semaphore_wait(barrier, len(partners))

    def send(src, slot, target):
        copy = pltpu.make_async_remote_copy(
            src_ref=src,
            dst_ref=xm if slot == XM else keys.at[slot],
            send_sem=send_sem.at[slot],
            recv_sem=recv_sem.at[slot],
            device_id=target,
            device_id_type=MESH,
        )
        copy.start()

    def arrived(dst, slot):
        pltpu.make_async_copy(dst, dst, recv_sem.at[slot]).wait()

    send(own, 0, (sibling, p))
    send(own, 1, (near, p))
    send(own, XM, (t, 1 - p))
    send(own, 3, (far, p))

    scaled = feat_ref[0].astype(f32) * (SCORE_SCALE * LOG2E)
    high = scaled.astype(bf16)
    low = (scaled - high.astype(f32)).astype(bf16)
    blank = jnp.zeros((CHANNELS, HALF), bf16)
    weights[0] = jnp.concatenate([high, blank, low, blank], axis=0)
    weights[1] = jnp.concatenate([blank, high, blank, low], axis=0)

    def step(u, carry):
        arrived(keys.at[u], u)

        @pl.when(u == 1)
        def _():
            send(keys.at[1], 2, (sibling, p))
            send(keys.at[1], 5, (across, p))

        @pl.when(u == 2)
        def _():
            arrived(xm, XM)
            send(xm, 7, (near, p))
            send(xm, 9, (far, p))
            send(xm, 6, (sibling, p))

        @pl.when(u == 3)
        def _():
            send(keys.at[3], 4, (sibling, p))

        @pl.when(u == 7)
        def _():
            send(keys.at[7], 8, (sibling, p))
            send(keys.at[7], 11, (across, p))

        @pl.when(u == 9)
        def _():
            send(keys.at[9], 10, (sibling, p))

        pltpu.make_async_copy(keys.at[u], kept_ref.at[u], keep_sem.at[u]).start()
        packed = keys[u, :PACK]
        packed = jnp.concatenate([packed, packed], axis=1)
        values = position_rows(keys[u, PACK:])
        highs, lows = [], []
        for half in range(2):
            scores = jnp.dot(packed, weights[half], preferred_element_type=f32)
            mass = jnp.exp2(scores)
            top = mass.astype(bf16)
            highs.append(top)
            lows.append((mass - top.astype(f32)).astype(bf16))
        acc[u] = jnp.dot(
            jnp.concatenate([values, values], axis=1),
            jnp.concatenate(highs + lows, axis=0),
            preferred_element_type=f32,
        )
        return carry

    lax.fori_loop(0, SLOTS, step, 0)

    coords = pos_ref[0].astype(f32)
    velocity = jnp.zeros((3, HALF), f32)
    sound = jnp.ones((1, HALF), f32)
    terms = jnp.minimum(REACH, total - 1 - t) + jnp.minimum(REACH, t)
    for slot, e in enumerate(OFFSETS):
        summed = acc[slot] + acc[slot + FRAME_SLOTS]
        den = summed[3:4]
        frame = t + e * sigma
        live = (frame >= 0) & (frame < total)
        fine = jnp.where((den > DEN_LOW) & (den < DEN_HIGH), 1.0, 0.0)
        sound = jnp.where(live, jnp.minimum(sound, fine), sound)
        share = sigma.astype(f32) / e
        velocity = velocity + jnp.where(live, (summed[:3] / den - coords) * share, 0.0)
    out_ref[0:3] = jnp.where(usable, velocity / terms.astype(f32), 0.0)
    out_ref[3:4] = jnp.where(usable, sound, 1.0)
    out_ref[4:8] = jnp.zeros((4, HALF), f32)

    def drain(slot, carry):
        pltpu.make_async_copy(keys.at[slot], kept_ref.at[slot], keep_sem.at[slot]).wait()
        pltpu.make_async_copy(own, own, send_sem.at[slot]).wait()
        return carry

    lax.fori_loop(0, SLOTS, drain, 0)
    pltpu.make_async_copy(own, own, send_sem.at[XM]).wait()


def finish(total, place_ref, cnt_ref, fast_ref, feat_ref, pos_ref, kept_ref, out_ref, feat, pos, block, stats, sem):
    sound = jnp.min(fast_ref[3:4]) > 0.5

    @pl.when(sound)
    def _():
        out_ref[0] = fast_ref[0:3]

    @pl.when(jnp.logical_not(sound))
    def _():
        t = place_ref[0]
        p = place_ref[1]
        sigma = 1 - 2 * lax.rem(t, 2)
        for src, dst in ((feat_ref, feat), (pos_ref, pos)):
            copy = pltpu.make_async_copy(src, dst, sem)
            copy.start()
            copy.wait()
        coords = pos[0].astype(f32)
        blank = jnp.zeros((CHANNELS, HALF), bf16)
        usable = lax.broadcasted_iota(jnp.int32, (1, HALF), 1) + p * HALF < cnt_ref[t]
        out_ref[0] = jnp.zeros((3, HALF), f32)
        terms = jnp.minimum(REACH, total - 1 - t) + jnp.minimum(REACH, t)

        def neighbour(slot, carry):
            size = jnp.where(slot < 2, slot + 1, jnp.where(slot < 4, slot - 1, 3))
            e = jnp.where((slot == 2) | (slot == 3) | (slot == 5), -size, size)
            frame = t + e * sigma
            live = (frame >= 0) & (frame < total)
            count = cnt_ref[wrapped(frame, total)]
            stats[0:8] = jnp.full((8, HALF), -1e30, f32)
            stats[8:16] = jnp.zeros((8, HALF), f32)

            def half_step(side, carry):
                copy = pltpu.make_async_copy(kept_ref.at[slot + side * FRAME_SLOTS], block, sem)
                copy.start()
                copy.wait()
                first = jnp.where(side == 0, p, 1 - p) * HALF
                values = position_rows(block[PACK:])
                for part in range(2):
                    query = [feat[0], blank] if part == 0 else [blank, feat[0]]
                    scores = (
                        jnp.dot(block[:PACK], jnp.concatenate(query, axis=0), preferred_element_type=f32)
                        * SCORE_SCALE
                    )
                    index = lax.broadcasted_iota(jnp.int32, (PACK, HALF), 0) + first + part * PACK
                    there = index < count
                    before = stats[0:1]
                    peak = jnp.maximum(before, jnp.max(jnp.where(there, scores, -1e30), axis=0, keepdims=True))
                    mass = jnp.where(there, jnp.exp(scores - peak), 0.0)
                    top = mass.astype(bf16)
                    rest = (mass - top.astype(f32)).astype(bf16)
                    lhs = values[:, part * PACK : (part + 1) * PACK]
                    fresh = jnp.dot(lhs, top, preferred_element_type=f32) + jnp.dot(
                        lhs, rest, preferred_element_type=f32
                    )
                    stats[8:16] = stats[8:16] * jnp.exp(before - peak) + fresh
                    stats[0:8] = jnp.broadcast_to(peak, (8, HALF))
                return carry

            lax.fori_loop(0, 2, half_step, 0)
            mean = stats[8:11] / stats[11:12]
            share = sigma.astype(f32) / e.astype(f32)
            out_ref[0] += jnp.where(live & usable, (mean - coords) * share, 0.0)
            return carry

        lax.fori_loop(0, FRAME_SLOTS, neighbour, 0)
        out_ref[0] = out_ref[0] / terms.astype(f32)


def per_device(features, positions, counts):
    total = counts.shape[0]
    vmem = pl.BlockSpec(memory_space=pltpu.VMEM)
    smem = pl.BlockSpec(memory_space=pltpu.SMEM)
    anywhere = pl.BlockSpec(memory_space=pl.ANY)
    fast, kept = pl.pallas_call(
        functools.partial(gather_and_match, total),
        out_shape=[
            jax.ShapeDtypeStruct((8, HALF), f32),
            jax.ShapeDtypeStruct((SLOTS, MSG, 128), bf16),
        ],
        in_specs=[smem, vmem, vmem],
        out_specs=[vmem, anywhere],
        scratch_shapes=[
            pltpu.VMEM((MSG, 128), bf16),
            pltpu.VMEM((MSG, 128), bf16),
            pltpu.VMEM((SLOTS, MSG, 128), bf16),
            pltpu.VMEM((2, 4 * CHANNELS, HALF), bf16),
            pltpu.VMEM((SLOTS, 8, HALF), f32),
            pltpu.SemaphoreType.DMA((SLOTS + 1,)),
            pltpu.SemaphoreType.DMA((SLOTS + 1,)),
            pltpu.SemaphoreType.DMA((SLOTS,)),
        ],
        compiler_params=pltpu.CompilerParams(
            collective_id=0, has_side_effects=True, vmem_limit_bytes=56 * 2**20
        ),
        name="gather_and_match",
    )(counts, features, positions)
    place = jnp.stack([lax.axis_index("tm"), lax.axis_index("pts")]).astype(jnp.int32)
    return pl.pallas_call(
        functools.partial(finish, total),
        out_shape=jax.ShapeDtypeStruct((1, 3, HALF), f32),
        in_specs=[smem, smem, vmem, anywhere, anywhere, anywhere],
        out_specs=vmem,
        scratch_shapes=[
            pltpu.VMEM((1, CHANNELS, HALF), bf16),
            pltpu.VMEM((1, 3, HALF), bf16),
            pltpu.VMEM((MSG, 128), bf16),
            pltpu.VMEM((16, HALF), f32),
            pltpu.SemaphoreType.DMA,
        ],
        compiler_params=pltpu.CompilerParams(vmem_limit_bytes=56 * 2**20),
        name="finish",
    )(place, counts, fast, features, positions, kept)


def solution(mesh):
    in_specs = (P("tm", None, "pts"), P("tm", None, "pts"), P())
    out_specs = P("tm", None, "pts")
    return jax.shard_map(
        per_device, mesh=mesh, in_specs=in_specs, out_specs=out_specs, check_vma=False
    )
```

time: 181 us -> 86.6 us (0.48)
  the two profiles are of different devices: /device:TPU:449 before, /device:TPU:1 now
where the time goes in v1:
time: 86.6 us; the launch traced here: 86.1 us
  Pallas kernels  84.1 us (97%)
  local copies, waits for them, and re-layouts  1.33 us (2%)
    pallas_call x1, Pallas kernels, per_device(): pl.pallas_call(functools.partial(finish, total), out_shape=jax.ShapeDtype...  45.8 us
    pallas_call x1, Pallas kernels, per_device(): pl.pallas_call(functools.partial(gather_and_match, total), out_shape=[jax...  38.2 us

profile of v1, /device:TPU:1, one launch (start us, length us, event | category | flops | bytes accessed | tf_op | source)
XLA Modules:
  0.0 86.1 jit_solution(7020931951737276014)
XLA Ops:
  0.0 0.6 pad_add_fusion.place_ref
  0.6 38.2 %gather_and_match.1 = (f32[8,1024]{1,0:T(8,128)}, bf16[12,544,128]{2,1,0:T(8,128)(2,1)}) custom-call(s32[256]{0:T(256)} %cnt_ref.3, bf16[1,64,1024]{2,1,0:T(8,128)(2,1)} %feat_ref.3, bf16[1,3,1024]{2,1,0:T(4,128)(2,1)} %pos_ref.3), custom_call_target="tpu_custom_call" | custom-call | tf_op jit(solution)/shard_map/gather_and_match/pallas_call | solution.py:250
  38.9 45.8 %finish.1 = f32[1,3,1024]{2,1,0:T(4,128)} custom-call(s32[2]{0:T(128)} %pad_add_fusion.place_ref, s32[256]{0:T(256)} %cnt_ref.3, f32[8,1024]{1,0:T(8,128)} %get-tuple-element.7.fast_ref, bf16[1,64,1024]{2,1,0:T(8,128)(2,1)} %feat_ref.3, bf16[1,3,1024]{2,1,0:T(4,128)(2,1)} %pos_ref.3, bf16[12,544,128]{2,1,0:T(8,128)(2,1)} %get-tuple-element.8.kept_ref), custom_call_target="tpu_custom_call" | custom-call | tf_op jit(solution)/shard_map/finish/pallas_call | solution.py:274
  84.7 1.3 %copy.4 = f32[1,3,1024]{2,0,1:T(1,128)} copy(f32[1,3,1024]{2,1,0:T(4,128)} %finish.1) | data formatting | bytes 24576 | tf_op jit(solution)/shard_map/finish/pallas_call | solution.py:274

commit v2 on v1

--- a/solution.py
+++ b/solution.py
@@ -27,8 +27,8 @@
 XM = SLOTS
 
 
-def wrapped(frame, total):
-    return lax.rem(frame + total, total)
+def inside(frame, total):
+    return (frame >= 0) & (frame < total)
 
 
 def pack_message(feat, pos, usable):
@@ -56,15 +56,18 @@
     t = lax.axis_index("tm")
     p = lax.axis_index("pts")
     sigma = 1 - 2 * lax.rem(t, 2)
-    sibling = wrapped(t + sigma, total)
-    across = wrapped(t - sigma, total)
-    near = wrapped(t - 2 * sigma, total)
-    far = wrapped(t + 2 * sigma, total)
-    partners = [(t, 1 - p), (sibling, p), (across, p), (near, p), (far, p)]
+    sibling, across, near, far = t + sigma, t - sigma, t - 2 * sigma, t + 2 * sigma
 
     barrier = pltpu.get_barrier_semaphore()
-    for partner in partners:
-        pl.semaphore_signal(barrier, inc=1, device_id=partner, device_id_type=MESH)
+    pl.semaphore_signal(barrier, inc=1, device_id=(t, 1 - p), device_id_type=MESH)
+    pl.semaphore_signal(barrier, inc=1, device_id=(sibling, p), device_id_type=MESH)
+    partners = 2
+    for frame in (across, near, far):
+        partners = partners + inside(frame, total).astype(jnp.int32)
+
+        @pl.when(inside(frame, total))
+        def _():
+            pl.semaphore_signal(barrier, inc=1, device_id=(frame, p), device_id_type=MESH)
 
     point = lax.broadcasted_iota(jnp.int32, (1, HALF), 1) + p * HALF
     usable = point < cnt_ref[t]
@@ -72,26 +75,27 @@
     own[:PACK] = rows
     own[PACK:] = tail
 
-    pl.semaphore_wait(barrier, len(partners))
-
-    def send(src, slot, target):
-        copy = pltpu.make_async_remote_copy(
-            src_ref=src,
-            dst_ref=xm if slot == XM else keys.at[slot],
-            send_sem=send_sem.at[slot],
-            recv_sem=recv_sem.at[slot],
-            device_id=target,
-            device_id_type=MESH,
-        )
-        copy.start()
+    pl.semaphore_wait(barrier, partners)
+
+    def send(src, slot, frame, half):
+        @pl.when(inside(frame, total))
+        def _():
+            pltpu.make_async_remote_copy(
+                src_ref=src,
+                dst_ref=xm if slot == XM else keys.at[slot],
+                send_sem=send_sem.at[slot],
+                recv_sem=recv_sem.at[slot],
+                device_id=(frame, half),
+                device_id_type=MESH,
+            ).start()
 
     def arrived(dst, slot):
         pltpu.make_async_copy(dst, dst, recv_sem.at[slot]).wait()
 
-    send(own, 0, (sibling, p))
-    send(own, 1, (near, p))
-    send(own, XM, (t, 1 - p))
-    send(own, 3, (far, p))
+    send(own, 0, sibling, p)
+    send(own, 1, near, p)
+    send(own, XM, t, 1 - p)
+    send(own, 3, far, p)
 
     scaled = feat_ref[0].astype(f32) * (SCORE_SCALE * LOG2E)
     high = scaled.astype(bf16)
@@ -100,33 +104,45 @@
     weights[0] = jnp.concatenate([high, blank, low, blank], axis=0)
     weights[1] = jnp.concatenate([blank, high, blank, low], axis=0)
 
+    def frame_of(slot):
+        place = lax.rem(slot, FRAME_SLOTS)
+        size = jnp.where(place < 2, place + 1, jnp.where(place < 4, place - 1, 3))
+        return t + sigma * jnp.where((place == 2) | (place == 3) | (place == 5), -size, size)
+
     def step(u, carry):
+        @pl.when(u == 2)
+        def _():
+            arrived(xm, XM)
+            send(xm, 7, near, p)
+            send(xm, 9, far, p)
+            send(xm, 6, sibling, p)
+
+        @pl.when(inside(frame_of(u), total))
+        def _():
+            match(u)
+
+        return carry
+
+    def match(u):
         arrived(keys.at[u], u)
 
         @pl.when(u == 1)
         def _():
-            send(keys.at[1], 2, (sibling, p))
-            send(keys.at[1], 5, (across, p))
-
-        @pl.when(u == 2)
-        def _():
-            arrived(xm, XM)
-            send(xm, 7, (near, p))
-            send(xm, 9, (far, p))
-            send(xm, 6, (sibling, p))
+            send(keys.at[1], 2, sibling, p)
+            send(keys.at[1], 5, across, p)
 
         @pl.when(u == 3)
         def _():
-            send(keys.at[3], 4, (sibling, p))
+            send(keys.at[3], 4, sibling, p)
 
         @pl.when(u == 7)
         def _():
-            send(keys.at[7], 8, (sibling, p))
-            send(keys.at[7], 11, (across, p))
+            send(keys.at[7], 8, sibling, p)
+            send(keys.at[7], 11, across, p)
 
         @pl.when(u == 9)
         def _():
-            send(keys.at[9], 10, (sibling, p))
+            send(keys.at[9], 10, sibling, p)
 
         pltpu.make_async_copy(keys.at[u], kept_ref.at[u], keep_sem.at[u]).start()
         packed = keys[u, :PACK]
@@ -144,7 +160,6 @@
             jnp.concatenate(highs + lows, axis=0),
             preferred_element_type=f32,
         )
-        return carry
 
     lax.fori_loop(0, SLOTS, step, 0)
 
@@ -155,8 +170,7 @@
     for slot, e in enumerate(OFFSETS):
         summed = acc[slot] + acc[slot + FRAME_SLOTS]
         den = summed[3:4]
-        frame = t + e * sigma
-        live = (frame >= 0) & (frame < total)
+        live = inside(t + e * sigma, total)
         fine = jnp.where((den > DEN_LOW) & (den < DEN_HIGH), 1.0, 0.0)
         sound = jnp.where(live, jnp.minimum(sound, fine), sound)
         share = sigma.astype(f32) / e
@@ -166,25 +180,46 @@
     out_ref[4:8] = jnp.zeros((4, HALF), f32)
 
     def drain(slot, carry):
-        pltpu.make_async_copy(keys.at[slot], kept_ref.at[slot], keep_sem.at[slot]).wait()
-        pltpu.make_async_copy(own, own, send_sem.at[slot]).wait()
+        @pl.when(inside(frame_of(slot), total))
+        def _():
+            pltpu.make_async_copy(keys.at[slot], kept_ref.at[slot], keep_sem.at[slot]).wait()
+
         return carry
 
     lax.fori_loop(0, SLOTS, drain, 0)
-    pltpu.make_async_copy(own, own, send_sem.at[XM]).wait()
-
-
-def finish(total, place_ref, cnt_ref, fast_ref, feat_ref, pos_ref, kept_ref, out_ref, feat, pos, block, stats, sem):
+
+    def sent(slot, frame, condition=True):
+        @pl.when(inside(frame, total) & condition)
+        def _():
+            pltpu.make_async_copy(own, own, send_sem.at[slot]).wait()
+
+    ahead = inside(far, total)
+    for side in (0, FRAME_SLOTS):
+        sent(side + 0, sibling)
+        sent(side + 1, near)
+        sent(side + 3, far)
+        sent(side + 2, sibling, ahead)
+        sent(side + 5, across, ahead)
+        sent(side + 4, sibling, inside(near, total))
+    sent(XM, t)
+
+
+def finish(total, cnt_ref, fast_ref, feat_ref, pos_ref, kept_ref, out_ref, feat, pos, block, stats, result, sem):
     sound = jnp.min(fast_ref[3:4]) > 0.5
+
+    def put(values):
+        for row in range(3):
+            for q in range(HALF // 128):
+                out_ref[row * 8 + q : row * 8 + q + 1] = values[row : row + 1, q * 128 : (q + 1) * 128]
 
     @pl.when(sound)
     def _():
-        out_ref[0] = fast_ref[0:3]
+        put(fast_ref[0:3])
 
     @pl.when(jnp.logical_not(sound))
     def _():
-        t = place_ref[0]
-        p = place_ref[1]
+        t = lax.axis_index("tm")
+        p = lax.axis_index("pts")
         sigma = 1 - 2 * lax.rem(t, 2)
         for src, dst in ((feat_ref, feat), (pos_ref, pos)):
             copy = pltpu.make_async_copy(src, dst, sem)
@@ -193,15 +228,15 @@
         coords = pos[0].astype(f32)
         blank = jnp.zeros((CHANNELS, HALF), bf16)
         usable = lax.broadcasted_iota(jnp.int32, (1, HALF), 1) + p * HALF < cnt_ref[t]
-        out_ref[0] = jnp.zeros((3, HALF), f32)
+        result[...] = jnp.zeros((8, HALF), f32)
         terms = jnp.minimum(REACH, total - 1 - t) + jnp.minimum(REACH, t)
 
         def neighbour(slot, carry):
             size = jnp.where(slot < 2, slot + 1, jnp.where(slot < 4, slot - 1, 3))
             e = jnp.where((slot == 2) | (slot == 3) | (slot == 5), -size, size)
             frame = t + e * sigma
-            live = (frame >= 0) & (frame < total)
-            count = cnt_ref[wrapped(frame, total)]
+            live = inside(frame, total)
+            count = cnt_ref[jnp.clip(frame, 0, total - 1)]
             stats[0:8] = jnp.full((8, HALF), -1e30, f32)
             stats[8:16] = jnp.zeros((8, HALF), f32)
 
@@ -235,11 +270,11 @@
             lax.fori_loop(0, 2, half_step, 0)
             mean = stats[8:11] / stats[11:12]
             share = sigma.astype(f32) / e.astype(f32)
-            out_ref[0] += jnp.where(live & usable, (mean - coords) * share, 0.0)
+            result[0:3] += jnp.where(live & usable, (mean - coords) * share, 0.0)
             return carry
 
         lax.fori_loop(0, FRAME_SLOTS, neighbour, 0)
-        out_ref[0] = out_ref[0] / terms.astype(f32)
+        put(result[0:3] / terms.astype(f32))
 
 
 def per_device(features, positions, counts):
@@ -270,22 +305,23 @@
         ),
         name="gather_and_match",
     )(counts, features, positions)
-    place = jnp.stack([lax.axis_index("tm"), lax.axis_index("pts")]).astype(jnp.int32)
-    return pl.pallas_call(
+    flat = pl.pallas_call(
         functools.partial(finish, total),
-        out_shape=jax.ShapeDtypeStruct((1, 3, HALF), f32),
-        in_specs=[smem, smem, vmem, anywhere, anywhere, anywhere],
+        out_shape=jax.ShapeDtypeStruct((3 * HALF // 128, 128), f32),
+        in_specs=[smem, vmem, anywhere, anywhere, anywhere],
         out_specs=vmem,
         scratch_shapes=[
             pltpu.VMEM((1, CHANNELS, HALF), bf16),
             pltpu.VMEM((1, 3, HALF), bf16),
             pltpu.VMEM((MSG, 128), bf16),
             pltpu.VMEM((16, HALF), f32),
+            pltpu.VMEM((8, HALF), f32),
             pltpu.SemaphoreType.DMA,
         ],
         compiler_params=pltpu.CompilerParams(vmem_limit_bytes=56 * 2**20),
         name="finish",
-    )(place, counts, fast, features, positions, kept)
+    )(counts, fast, features, positions, kept)
+    return flat.reshape(1, 3, HALF)
 
 
 def solution(mesh):

time: 86.6 us -> 80.2 us (0.926)
  the two profiles are of different devices: /device:TPU:1 before, /device:TPU:449 now
where the time goes in v2:
time: 80.2 us; the launch traced here: 79.8 us
  Pallas kernels  79.7 us (99%)
    pallas_call x1, Pallas kernels, per_device(): pl.pallas_call(functools.partial(finish, total), out_shape=jax.ShapeDtype...  45.9 us
    pallas_call x1, Pallas kernels, per_device(): pl.pallas_call(functools.partial(gather_and_match, total), out_shape=[jax...  33.8 us

profile of v2, /device:TPU:449, one launch (start us, length us, event | category | flops | bytes accessed | tf_op | source)
XLA Modules:
  0.0 79.8 jit_solution(14615885189192931579)
XLA Ops:
  0.0 33.8 %gather_and_match.1 = (f32[8,1024]{1,0:T(8,128)}, bf16[12,544,128]{2,1,0:T(8,128)(2,1)}) custom-call(s32[256]{0:T(256)} %cnt_ref.3, bf16[1,64,1024]{2,1,0:T(8,128)(2,1)} %feat_ref.3, bf16[1,3,1024]{2,1,0:T(4,128)(2,1)} %pos_ref.3), custom_call_target="tpu_custom_call" | custom-call | tf_op jit(solution)/shard_map/gather_and_match/pallas_call | solution.py:285
  33.8 45.9 %finish.1 = f32[24,128]{1,0:T(8,128)} custom-call(s32[256]{0:T(256)} %cnt_ref.3, f32[8,1024]{1,0:T(8,128)} %get-tuple-element.7.fast_ref, bf16[1,64,1024]{2,1,0:T(8,128)(2,1)} %feat_ref.3, bf16[1,3,1024]{2,1,0:T(4,128)(2,1)} %pos_ref.3, bf16[12,544,128]{2,1,0:T(8,128)(2,1)} %get-tuple-element.8.kept_ref), custom_call_target="tpu_custom_call" | custom-call | tf_op jit(solution)/shard_map/finish/pallas_call | solution.py:308

commit v3 on v2

--- a/solution.py
+++ b/solution.py
@@ -15,29 +15,57 @@
 MSG = PACK + POS_ROWS
 SCORE_SCALE = 0.25
 LOG2E = 1.4426950408889634
-DEN_LOW = 2.0**-90
-DEN_HIGH = 2.0**100
+DEN_LOW = 2.0**6
+DEN_HIGH = 2.0**24
+ROW_FRAMES = 16
 MESH = pl.DeviceIdType.MESH
 f32 = jnp.float32
 bf16 = jnp.bfloat16
-
-OFFSETS = (1, 2, -1, -2, 3, -3)
+f8 = jnp.float8_e5m2
+
+OFFSETS = (1, 2, -2, -1, 3, -3)
 FRAME_SLOTS = len(OFFSETS)
 SLOTS = 2 * FRAME_SLOTS
 XM = SLOTS
+ORDERS = (
+    (0, 1, 2, 3, 4, 5, 6, 7, 8, 9, 10, 11),
+    (0, 1, 4, 6, 7, 10, 2, 3, 5, 8, 9, 11),
+    (0, 2, 3, 5, 8, 6, 9, 11, 1, 4, 7, 10),
+    (0, 1, 2, 3, 4, 6, 7, 8, 9, 10, 5, 11),
+    (0, 1, 4, 6, 7, 10, 2, 3, 5, 8, 9, 11),
+)
+RELAY_STEPS = {
+    1: (1, 1, 5, 1, 1),
+    2: (2, 6, 1, 2, 6),
+    XM: (2, 2, 2, 2, 4),
+    7: (7, 4, 8, 6, 4),
+    8: (7, 9, 4, 7, 9),
+}
+CROSS_STEP = 1
 
 
 def inside(frame, total):
     return (frame >= 0) & (frame < total)
 
 
+def pick(table, place):
+    value = jnp.int32(table[-1])
+    for index, entry in enumerate(table[:-1]):
+        value = jnp.where(place == index, entry, value)
+    return value
+
+
+def other_row(a, b):
+    return lax.div(a, ROW_FRAMES) != lax.div(b, ROW_FRAMES)
+
+
 def pack_message(feat, pos, usable):
     kept = jnp.where(usable, feat.astype(f32), 0.0)
-    rows = jnp.concatenate([kept[:, :PACK], kept[:, PACK:]], axis=0).T
+    rows = jnp.concatenate([kept[:, :PACK], kept[:, PACK:]], axis=0).astype(bf16).T
     flag = usable.astype(f32)
     quad = jnp.concatenate([jnp.where(usable, pos.astype(f32), 0.0), flag], axis=0)
     tail = jnp.concatenate([quad[:, q * 128 : (q + 1) * 128] for q in range(HALF // 128)], axis=0)
-    return rows.astype(bf16), tail.astype(bf16)
+    return rows, tail.astype(bf16)
 
 
 def position_rows(tail):
@@ -51,38 +79,71 @@
 
 
 def gather_and_match(
-    total, cnt_ref, feat_ref, pos_ref, out_ref, kept_ref, own, xm, keys, weights, acc, send_sem, recv_sem, keep_sem
+    total,
+    cnt_ref,
+    feat_in,
+    pos_in,
+    out_ref,
+    kept_ref,
+    feat_ref,
+    pos_ref,
+    own,
+    xm,
+    keys,
+    weights,
+    acc,
+    send_sem,
+    recv_sem,
+    keep_sem,
+    load_sem,
 ):
     t = lax.axis_index("tm")
     p = lax.axis_index("pts")
     sigma = 1 - 2 * lax.rem(t, 2)
     sibling, across, near, far = t + sigma, t - sigma, t - 2 * sigma, t + 2 * sigma
 
+    loads = [
+        pltpu.make_async_copy(feat_in, feat_ref, load_sem.at[0]),
+        pltpu.make_async_copy(pos_in, pos_ref, load_sem.at[1]),
+    ]
+    for load in loads:
+        load.start()
+
     barrier = pltpu.get_barrier_semaphore()
     pl.semaphore_signal(barrier, inc=1, device_id=(t, 1 - p), device_id_type=MESH)
     pl.semaphore_signal(barrier, inc=1, device_id=(sibling, p), device_id_type=MESH)
     partners = 2
     for frame in (across, near, far):
-        partners = partners + inside(frame, total).astype(jnp.int32)
-
-        @pl.when(inside(frame, total))
+        there = inside(frame, total)
+        crossing = there & other_row(t, frame)
+        partners = partners + there.astype(jnp.int32) + crossing.astype(jnp.int32)
+
+        @pl.when(there)
         def _():
             pl.semaphore_signal(barrier, inc=1, device_id=(frame, p), device_id_type=MESH)
+
+        @pl.when(crossing)
+        def _():
+            pl.semaphore_signal(barrier, inc=1, device_id=(frame, 1 - p), device_id_type=MESH)
 
     point = lax.broadcasted_iota(jnp.int32, (1, HALF), 1) + p * HALF
     usable = point < cnt_ref[t]
+    for load in loads:
+        load.wait()
     rows, tail = pack_message(feat_ref[0], pos_ref[0], usable)
     own[:PACK] = rows
     own[PACK:] = tail
 
     pl.semaphore_wait(barrier, partners)
 
-    def send(src, slot, frame, half):
-        @pl.when(inside(frame, total))
+    def send(src, slot, frame, half, condition=True):
+        dst = xm if slot == XM else keys.at[slot]
+
+        @pl.when(inside(frame, total) & condition)
         def _():
             pltpu.make_async_remote_copy(
                 src_ref=src,
-                dst_ref=xm if slot == XM else keys.at[slot],
+                dst_ref=dst,
                 send_sem=send_sem.at[slot],
                 recv_sem=recv_sem.at[slot],
                 device_id=(frame, half),
@@ -92,73 +153,91 @@
     def arrived(dst, slot):
         pltpu.make_async_copy(dst, dst, recv_sem.at[slot]).wait()
 
+    near_crosses, far_crosses, across_crosses = (other_row(t, frame) for frame in (near, far, across))
     send(own, 0, sibling, p)
-    send(own, 1, near, p)
+    send(own, 1, near, p, jnp.logical_not(near_crosses))
+    send(own, 2, far, p, jnp.logical_not(far_crosses))
     send(own, XM, t, 1 - p)
-    send(own, 3, far, p)
 
     scaled = feat_ref[0].astype(f32) * (SCORE_SCALE * LOG2E)
     high = scaled.astype(bf16)
     low = (scaled - high.astype(f32)).astype(bf16)
-    blank = jnp.zeros((CHANNELS, HALF), bf16)
-    weights[0] = jnp.concatenate([high, blank, low, blank], axis=0)
-    weights[1] = jnp.concatenate([blank, high, blank, low], axis=0)
+    weights[...] = jnp.concatenate([high, low], axis=0)
 
     def frame_of(slot):
         place = lax.rem(slot, FRAME_SLOTS)
-        size = jnp.where(place < 2, place + 1, jnp.where(place < 4, place - 1, 3))
-        return t + sigma * jnp.where((place == 2) | (place == 3) | (place == 5), -size, size)
-
-    def step(u, carry):
-        @pl.when(u == 2)
-        def _():
-            arrived(xm, XM)
-            send(xm, 7, near, p)
-            send(xm, 9, far, p)
-            send(xm, 6, sibling, p)
+        return t + sigma * pick(OFFSETS, place)
+
+    place = lax.rem(t, ROW_FRAMES)
+    mirrored = jnp.minimum(place, ROW_FRAMES - 1 - place)
+    kind = jnp.where(mirrored < 3, mirrored + 1, 0)
+    kind = jnp.where(lax.rem(t, 2 * ROW_FRAMES) == 0, 4, kind)
+
+    def relay(step, slot):
+        due = step == pick(RELAY_STEPS[slot], kind)
+        if slot == XM:
+
+            @pl.when(due)
+            def _():
+                arrived(xm, XM)
+                send(xm, 6, sibling, p)
+                send(xm, 7, near, p, jnp.logical_not(near_crosses))
+                send(xm, 8, far, p, jnp.logical_not(far_crosses))
+                send(own, 7, near, 1 - p, near_crosses)
+                send(own, 8, far, 1 - p, far_crosses)
+
+            return
+
+        @pl.when(due & inside(frame_of(slot), total))
+        def _():
+            arrived(keys.at[slot], slot)
+            if slot in (1, 7):
+                send(keys.at[slot], slot + 2, sibling, p)
+                send(keys.at[slot], slot + 4, across, p, True if slot == 1 else jnp.logical_not(across_crosses))
+                if slot == 1:
+                    send(keys.at[slot], 11, across, 1 - p, across_crosses)
+            else:
+                send(keys.at[slot], slot + 2, sibling, p)
+
+    def step(index, carry):
+        @pl.when(index == CROSS_STEP)
+        def _():
+            send(own, 1, near, p, near_crosses)
+            send(own, 2, far, p, far_crosses)
+
+        for slot in RELAY_STEPS:
+            relay(index, slot)
+
+        u = jnp.int32(0)
+        for which, order in enumerate(ORDERS):
+            u = jnp.where(kind == which, pick(order, index), u)
 
         @pl.when(inside(frame_of(u), total))
         def _():
+            @pl.when((u != 1) & (u != 2) & (u != 7) & (u != 8))
+            def _():
+                arrived(keys.at[u], u)
+
             match(u)
 
         return carry
 
     def match(u):
-        arrived(keys.at[u], u)
-
-        @pl.when(u == 1)
-        def _():
-            send(keys.at[1], 2, sibling, p)
-            send(keys.at[1], 5, across, p)
-
-        @pl.when(u == 3)
-        def _():
-            send(keys.at[3], 4, sibling, p)
-
-        @pl.when(u == 7)
-        def _():
-            send(keys.at[7], 8, sibling, p)
-            send(keys.at[7], 11, across, p)
-
-        @pl.when(u == 9)
-        def _():
-            send(keys.at[9], 10, sibling, p)
-
         pltpu.make_async_copy(keys.at[u], kept_ref.at[u], keep_sem.at[u]).start()
-        packed = keys[u, :PACK]
-        packed = jnp.concatenate([packed, packed], axis=1)
+        packed = keys[u, :PACK].astype(f32)
+        turned = pltpu.roll(packed, CHANNELS, 1)
+        left = lax.broadcasted_iota(jnp.int32, (PACK, 2 * CHANNELS), 1) < CHANNELS
         values = position_rows(keys[u, PACK:])
         highs, lows = [], []
         for half in range(2):
-            scores = jnp.dot(packed, weights[half], preferred_element_type=f32)
+            points = jnp.where(left, packed, turned) if half == 0 else jnp.where(left, turned, packed)
+            scores = jnp.dot(points.astype(bf16), weights[...], preferred_element_type=f32)
             mass = jnp.exp2(scores)
             top = mass.astype(bf16)
             highs.append(top)
-            lows.append((mass - top.astype(f32)).astype(bf16))
-        acc[u] = jnp.dot(
-            jnp.concatenate([values, values], axis=1),
-            jnp.concatenate(highs + lows, axis=0),
-            preferred_element_type=f32,
+            lows.append((mass - top.astype(f32)).astype(f8))
+        acc[u] = jnp.dot(values, jnp.concatenate(highs, axis=0), preferred_element_type=f32) + jnp.dot(
+            values.astype(f8), jnp.concatenate(lows, axis=0), preferred_element_type=f32
         )
 
     lax.fori_loop(0, SLOTS, step, 0)
@@ -197,10 +276,10 @@
     for side in (0, FRAME_SLOTS):
         sent(side + 0, sibling)
         sent(side + 1, near)
-        sent(side + 3, far)
-        sent(side + 2, sibling, ahead)
+        sent(side + 2, far)
+        sent(side + 3, sibling, ahead)
+        sent(side + 4, sibling, inside(near, total))
         sent(side + 5, across, ahead)
-        sent(side + 4, sibling, inside(near, total))
     sent(XM, t)
 
 
@@ -232,8 +311,7 @@
         terms = jnp.minimum(REACH, total - 1 - t) + jnp.minimum(REACH, t)
 
         def neighbour(slot, carry):
-            size = jnp.where(slot < 2, slot + 1, jnp.where(slot < 4, slot - 1, 3))
-            e = jnp.where((slot == 2) | (slot == 3) | (slot == 5), -size, size)
+            e = pick(OFFSETS, slot)
             frame = t + e * sigma
             live = inside(frame, total)
             count = cnt_ref[jnp.clip(frame, 0, total - 1)]
@@ -288,17 +366,20 @@
             jax.ShapeDtypeStruct((8, HALF), f32),
             jax.ShapeDtypeStruct((SLOTS, MSG, 128), bf16),
         ],
-        in_specs=[smem, vmem, vmem],
+        in_specs=[smem, anywhere, anywhere],
         out_specs=[vmem, anywhere],
         scratch_shapes=[
+            pltpu.VMEM((1, CHANNELS, HALF), bf16),
+            pltpu.VMEM((1, 3, HALF), bf16),
             pltpu.VMEM((MSG, 128), bf16),
             pltpu.VMEM((MSG, 128), bf16),
             pltpu.VMEM((SLOTS, MSG, 128), bf16),
-            pltpu.VMEM((2, 4 * CHANNELS, HALF), bf16),
+            pltpu.VMEM((2 * CHANNELS, HALF), bf16),
             pltpu.VMEM((SLOTS, 8, HALF), f32),
             pltpu.SemaphoreType.DMA((SLOTS + 1,)),
             pltpu.SemaphoreType.DMA((SLOTS + 1,)),
             pltpu.SemaphoreType.DMA((SLOTS,)),
+            pltpu.SemaphoreType.DMA((2,)),
         ],
         compiler_params=pltpu.CompilerParams(
             collective_id=0, has_side_effects=True, vmem_limit_bytes=56 * 2**20

time: 80.2 us -> 75.2 us (0.938)
  Pallas kernels: 79.7 us -> 74.4 us
    pallas_call x1, Pallas kernels: 33.8 us -> 28.5 us  [per_device(): pl.pallas_call(functools.partial(gather_and_match, total), out_shape=[jax...]
where the time goes in v3:
time: 75.2 us; the launch traced here: 74.4 us
  Pallas kernels  74.4 us (99%)
    pallas_call x1, Pallas kernels, per_device(): pl.pallas_call(functools.partial(finish, total), out_shape=jax.ShapeDtype...  45.9 us
    pallas_call x1, Pallas kernels, per_device(): pl.pallas_call(functools.partial(gather_and_match, total), out_shape=[jax...  28.5 us

profile of v3, /device:TPU:449, one launch (start us, length us, event | category | flops | bytes accessed | tf_op | source)
XLA Modules:
  0.0 74.4 jit_solution(13326887557096284568)
XLA Ops:
  0.0 28.5 %gather_and_match.1 = (f32[8,1024]{1,0:T(8,128)}, bf16[12,544,128]{2,1,0:T(8,128)(2,1)}) custom-call(s32[256]{0:T(256)} %cnt_ref.3, bf16[1,64,1024]{2,1,0:T(8,128)(2,1)} %feat_ref.1, bf16[1,3,1024]{2,1,0:T(4,128)(2,1)} %pos_ref.1), custom_call_target="tpu_custom_call" | custom-call | tf_op jit(solution)/shard_map/gather_and_match/pallas_call | solution.py:363
  28.5 45.9 %finish.1 = f32[24,128]{1,0:T(8,128)} custom-call(s32[256]{0:T(256)} %cnt_ref.3, f32[8,1024]{1,0:T(8,128)} %get-tuple-element.7.fast_ref, bf16[1,64,1024]{2,1,0:T(8,128)(2,1)} %feat_ref.1, bf16[1,3,1024]{2,1,0:T(4,128)(2,1)} %pos_ref.1, bf16[12,544,128]{2,1,0:T(8,128)(2,1)} %get-tuple-element.8.kept_ref), custom_call_target="tpu_custom_call" | custom-call | tf_op jit(solution)/shard_map/finish/pallas_call | solution.py:389

commit v4 on v3

--- a/solution.py
+++ b/solution.py
@@ -30,17 +30,19 @@
 ORDERS = (
     (0, 1, 2, 3, 4, 5, 6, 7, 8, 9, 10, 11),
     (0, 1, 4, 6, 7, 10, 2, 3, 5, 8, 9, 11),
-    (0, 2, 3, 5, 8, 6, 9, 11, 1, 4, 7, 10),
+    (0, 2, 3, 6, 5, 8, 1, 9, 4, 7, 10, 11),
     (0, 1, 2, 3, 4, 6, 7, 8, 9, 10, 5, 11),
-    (0, 1, 4, 6, 7, 10, 2, 3, 5, 8, 9, 11),
+    (0, 2, 3, 6, 5, 8, 9, 1, 7, 4, 11, 10),
 )
+KINDS = (1, 2, 3, 0, 0, 0, 0, 0, 0, 0, 0, 0, 0, 3, 4, 1)
 RELAY_STEPS = {
-    1: (1, 1, 5, 1, 1),
-    2: (2, 6, 1, 2, 6),
-    XM: (2, 2, 2, 2, 4),
-    7: (7, 4, 8, 6, 4),
-    8: (7, 9, 4, 7, 9),
+    1: (1, 1, 5, 1, 7),
+    2: (2, 6, 1, 2, 1),
+    XM: (3, 3, 3, 3, 3),
+    7: (7, 4, 8, 6, 8),
+    8: (7, 8, 5, 7, 5),
 }
+BACK_STEP = 3
 CROSS_STEP = 1
 
 
@@ -80,11 +82,12 @@
 
 def gather_and_match(
     total,
-    cnt_ref,
+    cnt_in,
     feat_in,
     pos_in,
     out_ref,
     kept_ref,
+    cnt_ref,
     feat_ref,
     pos_ref,
     own,
@@ -96,6 +99,8 @@
     recv_sem,
     keep_sem,
     load_sem,
+    half_ready,
+    row_ready,
 ):
     t = lax.axis_index("tm")
     p = lax.axis_index("pts")
@@ -105,36 +110,57 @@
     loads = [
         pltpu.make_async_copy(feat_in, feat_ref, load_sem.at[0]),
         pltpu.make_async_copy(pos_in, pos_ref, load_sem.at[1]),
+        pltpu.make_async_copy(cnt_in, cnt_ref, load_sem.at[2]),
     ]
     for load in loads:
         load.start()
 
     barrier = pltpu.get_barrier_semaphore()
-    pl.semaphore_signal(barrier, inc=1, device_id=(t, 1 - p), device_id_type=MESH)
     pl.semaphore_signal(barrier, inc=1, device_id=(sibling, p), device_id_type=MESH)
-    partners = 2
+    awaited = 1 + p
+    above, below = jnp.int32(0), jnp.int32(0)
+
+    @pl.when(p == 0)
+    def _():
+        pl.semaphore_signal(barrier, inc=1, device_id=(t, 1 - p), device_id_type=MESH)
+
     for frame in (across, near, far):
         there = inside(frame, total)
         crossing = there & other_row(t, frame)
-        partners = partners + there.astype(jnp.int32) + crossing.astype(jnp.int32)
-
-        @pl.when(there)
+        same = there & jnp.logical_not(other_row(t, frame))
+        awaited = awaited + same.astype(jnp.int32)
+        above = above + (crossing & (frame > t)).astype(jnp.int32)
+        below = below + (crossing & (frame < t)).astype(jnp.int32)
+
+        @pl.when(same | (crossing & (frame < t)))
         def _():
             pl.semaphore_signal(barrier, inc=1, device_id=(frame, p), device_id_type=MESH)
 
-        @pl.when(crossing)
+        @pl.when(crossing & (frame < t))
         def _():
             pl.semaphore_signal(barrier, inc=1, device_id=(frame, 1 - p), device_id_type=MESH)
 
     point = lax.broadcasted_iota(jnp.int32, (1, HALF), 1) + p * HALF
-    usable = point < cnt_ref[t]
     for load in loads:
         load.wait()
+    usable = point < cnt_ref[t]
     rows, tail = pack_message(feat_ref[0], pos_ref[0], usable)
     own[:PACK] = rows
     own[PACK:] = tail
 
-    pl.semaphore_wait(barrier, partners)
+    pl.semaphore_wait(barrier, awaited + 2 * above)
+
+    @pl.when(p == 1)
+    def _():
+        pl.semaphore_signal(half_ready, inc=1, device_id=(t, 1 - p), device_id_type=MESH)
+
+    for frame in (across, near, far):
+
+        @pl.when(inside(frame, total) & other_row(t, frame) & (frame > t))
+        def _():
+            for half in (p, 1 - p):
+                pl.semaphore_signal(row_ready, inc=1, device_id=(frame, half), device_id_type=MESH)
+
 
     def send(src, slot, frame, half, condition=True):
         dst = xm if slot == XM else keys.at[slot]
@@ -157,7 +183,7 @@
     send(own, 0, sibling, p)
     send(own, 1, near, p, jnp.logical_not(near_crosses))
     send(own, 2, far, p, jnp.logical_not(far_crosses))
-    send(own, XM, t, 1 - p)
+    send(own, XM, t, 1 - p, p == 1)
 
     scaled = feat_ref[0].astype(f32) * (SCORE_SCALE * LOG2E)
     high = scaled.astype(bf16)
@@ -169,9 +195,7 @@
         return t + sigma * pick(OFFSETS, place)
 
     place = lax.rem(t, ROW_FRAMES)
-    mirrored = jnp.minimum(place, ROW_FRAMES - 1 - place)
-    kind = jnp.where(mirrored < 3, mirrored + 1, 0)
-    kind = jnp.where(lax.rem(t, 2 * ROW_FRAMES) == 0, 4, kind)
+    kind = pick(KINDS, place)
 
     def relay(step, slot):
         due = step == pick(RELAY_STEPS[slot], kind)
@@ -183,8 +207,8 @@
                 send(xm, 6, sibling, p)
                 send(xm, 7, near, p, jnp.logical_not(near_crosses))
                 send(xm, 8, far, p, jnp.logical_not(far_crosses))
-                send(own, 7, near, 1 - p, near_crosses)
-                send(own, 8, far, 1 - p, far_crosses)
+                send(own, 7, near, 1 - p, near_crosses & (near > t))
+                send(own, 8, far, 1 - p, far_crosses & (far > t))
 
             return
 
@@ -193,20 +217,38 @@
             arrived(keys.at[slot], slot)
             if slot in (1, 7):
                 send(keys.at[slot], slot + 2, sibling, p)
-                send(keys.at[slot], slot + 4, across, p, True if slot == 1 else jnp.logical_not(across_crosses))
                 if slot == 1:
-                    send(keys.at[slot], 11, across, 1 - p, across_crosses)
+                    ready = jnp.logical_not(across_crosses) | (across > t)
+                    send(keys.at[slot], 5, across, p, ready)
+                    send(keys.at[slot], 11, across, 1 - p, across_crosses & ready)
+                else:
+                    send(keys.at[slot], 11, across, p, jnp.logical_not(across_crosses))
             else:
                 send(keys.at[slot], slot + 2, sibling, p)
 
     def step(index, carry):
         @pl.when(index == CROSS_STEP)
         def _():
+            send(own, 1, near, p, near_crosses & (near > t))
+            send(own, 2, far, p, far_crosses & (far > t))
+
+        @pl.when((index == 0) & (p == 0))
+        def _():
+            pl.semaphore_wait(half_ready, 1)
+            send(own, XM, t, 1 - p)
+
+        for slot in RELAY_STEPS:
+            relay(index, slot)
+
+        @pl.when((index == BACK_STEP) & (below > 0))
+        def _():
+            pl.semaphore_wait(row_ready, 2 * below)
             send(own, 1, near, p, near_crosses)
             send(own, 2, far, p, far_crosses)
-
-        for slot in RELAY_STEPS:
-            relay(index, slot)
+            send(own, 7, near, 1 - p, near_crosses)
+            send(own, 8, far, 1 - p, far_crosses)
+            for slot, half in ((5, p), (11, 1 - p)):
+                send(keys.at[1], slot, across, half, across_crosses)
 
         u = jnp.int32(0)
         for which, order in enumerate(ORDERS):
@@ -366,9 +408,10 @@
             jax.ShapeDtypeStruct((8, HALF), f32),
             jax.ShapeDtypeStruct((SLOTS, MSG, 128), bf16),
         ],
-        in_specs=[smem, anywhere, anywhere],
+        in_specs=[anywhere, anywhere, anywhere],
         out_specs=[vmem, anywhere],
         scratch_shapes=[
+            pltpu.SMEM((total,), jnp.int32),
             pltpu.VMEM((1, CHANNELS, HALF), bf16),
             pltpu.VMEM((1, 3, HALF), bf16),
             pltpu.VMEM((MSG, 128), bf16),
@@ -379,7 +422,9 @@
             pltpu.SemaphoreType.DMA((SLOTS + 1,)),
             pltpu.SemaphoreType.DMA((SLOTS + 1,)),
             pltpu.SemaphoreType.DMA((SLOTS,)),
-            pltpu.SemaphoreType.DMA((2,)),
+            pltpu.SemaphoreType.DMA((3,)),
+            pltpu.SemaphoreType.REGULAR,
+            pltpu.SemaphoreType.REGULAR,
         ],
         compiler_params=pltpu.CompilerParams(
             collective_id=0, has_side_effects=True, vmem_limit_bytes=56 * 2**20

time: 75.2 us -> 74.3 us (0.988)
  the two profiles are of different devices: /device:TPU:449 before, /device:TPU:1 now
where the time goes in v4:
time: 74.3 us; the launch traced here: 73.8 us
  Pallas kernels  73.8 us (99%)
    pallas_call x1, Pallas kernels, per_device(): pl.pallas_call(functools.partial(finish, total), out_shape=jax.ShapeDtype...  45.9 us
    pallas_call x1, Pallas kernels, per_device(): pl.pallas_call(functools.partial(gather_and_match, total), out_shape=[jax...  27.8 us

profile of v4, /device:TPU:1, one launch (start us, length us, event | category | flops | bytes accessed | tf_op | source)
XLA Modules:
  0.0 73.8 jit_solution(5045905427189898604)
XLA Ops:
  0.0 27.8 %gather_and_match.1 = (f32[8,1024]{1,0:T(8,128)}, bf16[12,544,128]{2,1,0:T(8,128)(2,1)}) custom-call(s32[256]{0:T(256)} %cnt_ref.1, bf16[1,64,1024]{2,1,0:T(8,128)(2,1)} %feat_ref.1, bf16[1,3,1024]{2,1,0:T(4,128)(2,1)} %pos_ref.1), custom_call_target="tpu_custom_call" | custom-call | tf_op jit(solution)/shard_map/gather_and_match/pallas_call | solution.py:405
  27.9 45.9 %finish.1 = f32[24,128]{1,0:T(8,128)} custom-call(s32[256]{0:T(256)} %cnt_ref.1, f32[8,1024]{1,0:T(8,128)} %get-tuple-element.7.fast_ref, bf16[1,64,1024]{2,1,0:T(8,128)(2,1)} %feat_ref.1, bf16[1,3,1024]{2,1,0:T(4,128)(2,1)} %pos_ref.1, bf16[12,544,128]{2,1,0:T(8,128)(2,1)} %get-tuple-element.8.kept_ref), custom_call_target="tpu_custom_call" | custom-call | tf_op jit(solution)/shard_map/finish/pallas_call | solution.py:434

commit v5 on v4

--- a/solution.py
+++ b/solution.py
@@ -13,6 +13,8 @@
 PACK = HALF // 2
 POS_ROWS = 32
 MSG = PACK + POS_ROWS
+ROWS = 3 * HALF // 128
+FLAG_ROWS = HALF // 128
 SCORE_SCALE = 0.25
 LOG2E = 1.4426950408889634
 DEN_LOW = 2.0**6
@@ -29,18 +31,20 @@
 XM = SLOTS
 ORDERS = (
     (0, 1, 2, 3, 4, 5, 6, 7, 8, 9, 10, 11),
-    (0, 1, 4, 6, 7, 10, 2, 3, 5, 8, 9, 11),
+    (0, 1, 4, 6, 7, 10, 2, 3, 8, 5, 9, 11),
     (0, 2, 3, 6, 5, 8, 1, 9, 4, 7, 10, 11),
     (0, 1, 2, 3, 4, 6, 7, 8, 9, 10, 5, 11),
     (0, 2, 3, 6, 5, 8, 9, 1, 7, 4, 11, 10),
+    (0, 1, 4, 6, 7, 2, 10, 3, 8, 5, 9, 11),
+    (0, 2, 3, 5, 8, 6, 9, 11, 1, 4, 7, 10),
 )
-KINDS = (1, 2, 3, 0, 0, 0, 0, 0, 0, 0, 0, 0, 0, 3, 4, 1)
+KINDS = (1, 2, 3, 0, 0, 0, 0, 0, 0, 0, 0, 0, 0, 3, 4, 5)
 RELAY_STEPS = {
-    1: (1, 1, 5, 1, 7),
-    2: (2, 6, 1, 2, 1),
-    XM: (3, 3, 3, 3, 3),
-    7: (7, 4, 8, 6, 8),
-    8: (7, 8, 5, 7, 5),
+    1: (1, 1, 5, 1, 7, 1, 8),
+    2: (2, 6, 1, 2, 1, 5, 1),
+    XM: (3, 3, 3, 3, 3, 3, 3),
+    7: (7, 4, 8, 6, 8, 4, 10),
+    8: (7, 8, 5, 7, 5, 8, 4),
 }
 BACK_STEP = 3
 CROSS_STEP = 1
@@ -78,6 +82,13 @@
         pieces.append(block)
         pieces.append(jnp.concatenate([block[4:], block[:4]], axis=0))
     return jnp.concatenate(pieces, axis=1).astype(bf16)
+
+
+def put_rows(ref, values, first):
+    for row in range(values.shape[0]):
+        for q in range(HALF // 128):
+            at = first + row * (HALF // 128) + q
+            ref[at : at + 1] = values[row : row + 1, q * 128 : (q + 1) * 128]
 
 
 def gather_and_match(
@@ -101,6 +112,8 @@
     load_sem,
     half_ready,
     row_ready,
+    result,
+    result_sem,
 ):
     t = lax.axis_index("tm")
     p = lax.axis_index("pts")
@@ -195,7 +208,7 @@
         return t + sigma * pick(OFFSETS, place)
 
     place = lax.rem(t, ROW_FRAMES)
-    kind = pick(KINDS, place)
+    kind = jnp.where(t == 1, 6, pick(KINDS, place))
 
     def relay(step, slot):
         due = step == pick(RELAY_STEPS[slot], kind)
@@ -296,9 +309,10 @@
         sound = jnp.where(live, jnp.minimum(sound, fine), sound)
         share = sigma.astype(f32) / e
         velocity = velocity + jnp.where(live, (summed[:3] / den - coords) * share, 0.0)
-    out_ref[0:3] = jnp.where(usable, velocity / terms.astype(f32), 0.0)
-    out_ref[3:4] = jnp.where(usable, sound, 1.0)
-    out_ref[4:8] = jnp.zeros((4, HALF), f32)
+    put_rows(result, jnp.where(usable, velocity / terms.astype(f32), 0.0), 0)
+    put_rows(result, jnp.where(usable, sound, 1.0), ROWS)
+    leave = pltpu.make_async_copy(result, out_ref, result_sem)
+    leave.start()
 
     def drain(slot, carry):
         @pl.when(inside(frame_of(slot), total))
@@ -323,27 +337,27 @@
         sent(side + 4, sibling, inside(near, total))
         sent(side + 5, across, ahead)
     sent(XM, t)
-
-
-def finish(total, cnt_ref, fast_ref, feat_ref, pos_ref, kept_ref, out_ref, feat, pos, block, stats, result, sem):
-    sound = jnp.min(fast_ref[3:4]) > 0.5
-
-    def put(values):
-        for row in range(3):
-            for q in range(HALF // 128):
-                out_ref[row * 8 + q : row * 8 + q + 1] = values[row : row + 1, q * 128 : (q + 1) * 128]
-
-    @pl.when(sound)
-    def _():
-        put(fast_ref[0:3])
+    leave.wait()
+
+
+def finish(
+    total, cnt_in, fast_ref, feat_ref, pos_ref, kept_ref, out_ref, cnt_ref, flags, feat, pos, block, stats, result, lines, sem
+):
+    whole = pltpu.make_async_copy(fast_ref.at[pl.ds(0, ROWS)], out_ref, sem.at[0])
+    check = pltpu.make_async_copy(fast_ref.at[pl.ds(ROWS, FLAG_ROWS)], flags, sem.at[1])
+    check.start()
+    whole.start()
+    check.wait()
+    sound = jnp.min(flags[...]) > 0.5
+    whole.wait()
 
     @pl.when(jnp.logical_not(sound))
     def _():
         t = lax.axis_index("tm")
         p = lax.axis_index("pts")
         sigma = 1 - 2 * lax.rem(t, 2)
-        for src, dst in ((feat_ref, feat), (pos_ref, pos)):
-            copy = pltpu.make_async_copy(src, dst, sem)
+        for src, dst in ((feat_ref, feat), (pos_ref, pos), (cnt_in, cnt_ref)):
+            copy = pltpu.make_async_copy(src, dst, sem.at[0])
             copy.start()
             copy.wait()
         coords = pos[0].astype(f32)
@@ -361,7 +375,7 @@
             stats[8:16] = jnp.zeros((8, HALF), f32)
 
             def half_step(side, carry):
-                copy = pltpu.make_async_copy(kept_ref.at[slot + side * FRAME_SLOTS], block, sem)
+                copy = pltpu.make_async_copy(kept_ref.at[slot + side * FRAME_SLOTS], block, sem.at[0])
                 copy.start()
                 copy.wait()
                 first = jnp.where(side == 0, p, 1 - p) * HALF
@@ -394,22 +408,23 @@
             return carry
 
         lax.fori_loop(0, FRAME_SLOTS, neighbour, 0)
-        put(result[0:3] / terms.astype(f32))
+        put_rows(lines, result[0:3] / terms.astype(f32), 0)
+        copy = pltpu.make_async_copy(lines, out_ref, sem.at[0])
+        copy.start()
+        copy.wait()
 
 
 def per_device(features, positions, counts):
     total = counts.shape[0]
-    vmem = pl.BlockSpec(memory_space=pltpu.VMEM)
-    smem = pl.BlockSpec(memory_space=pltpu.SMEM)
     anywhere = pl.BlockSpec(memory_space=pl.ANY)
     fast, kept = pl.pallas_call(
         functools.partial(gather_and_match, total),
         out_shape=[
-            jax.ShapeDtypeStruct((8, HALF), f32),
+            jax.ShapeDtypeStruct((ROWS + FLAG_ROWS, 128), f32),
             jax.ShapeDtypeStruct((SLOTS, MSG, 128), bf16),
         ],
         in_specs=[anywhere, anywhere, anywhere],
-        out_specs=[vmem, anywhere],
+        out_specs=[anywhere, anywhere],
         scratch_shapes=[
             pltpu.SMEM((total,), jnp.int32),
             pltpu.VMEM((1, CHANNELS, HALF), bf16),
@@ -425,6 +440,8 @@
             pltpu.SemaphoreType.DMA((3,)),
             pltpu.SemaphoreType.REGULAR,
             pltpu.SemaphoreType.REGULAR,
+            pltpu.VMEM((ROWS + FLAG_ROWS, 128), f32),
+            pltpu.SemaphoreType.DMA,
         ],
         compiler_params=pltpu.CompilerParams(
             collective_id=0, has_side_effects=True, vmem_limit_bytes=56 * 2**20
@@ -434,15 +451,18 @@
     flat = pl.pallas_call(
         functools.partial(finish, total),
         out_shape=jax.ShapeDtypeStruct((3 * HALF // 128, 128), f32),
-        in_specs=[smem, vmem, anywhere, anywhere, anywhere],
-        out_specs=vmem,
+        in_specs=[anywhere] * 5,
+        out_specs=anywhere,
         scratch_shapes=[
+            pltpu.SMEM((total,), jnp.int32),
+            pltpu.VMEM((FLAG_ROWS, 128), f32),
             pltpu.VMEM((1, CHANNELS, HALF), bf16),
             pltpu.VMEM((1, 3, HALF), bf16),
             pltpu.VMEM((MSG, 128), bf16),
             pltpu.VMEM((16, HALF), f32),
             pltpu.VMEM((8, HALF), f32),
-            pltpu.SemaphoreType.DMA,
+            pltpu.VMEM((ROWS, 128), f32),
+            pltpu.SemaphoreType.DMA((2,)),
         ],
         compiler_params=pltpu.CompilerParams(vmem_limit_bytes=56 * 2**20),
         name="finish",

time: 74.3 us -> 74.9 us (level)
  the two profiles are of different devices: /device:TPU:1 before, /device:TPU:251 now
where the time goes in v5:
time: 74.9 us; the launch traced here: 74.4 us
  Pallas kernels  74.4 us (99%)
    pallas_call x1, Pallas kernels, per_device(): pl.pallas_call(functools.partial(finish, total), out_shape=jax.ShapeDtype...  47.2 us
    pallas_call x1, Pallas kernels, per_device(): pl.pallas_call(functools.partial(gather_and_match, total), out_shape=[jax...  27.2 us

profile of v5, /device:TPU:251, one launch (start us, length us, event | category | flops | bytes accessed | tf_op | source)
XLA Modules:
  0.0 74.4 jit_solution(11565709958537404073)
XLA Ops:
  0.0 27.2 %gather_and_match.1 = (f32[32,128]{1,0:T(8,128)}, bf16[12,544,128]{2,1,0:T(8,128)(2,1)}) custom-call(s32[256]{0:T(256)} %cnt_in.3, bf16[1,64,1024]{2,1,0:T(8,128)(2,1)} %feat_ref.1, bf16[1,3,1024]{2,1,0:T(4,128)(2,1)} %pos_ref.1), custom_call_target="tpu_custom_call" | custom-call | tf_op jit(solution)/shard_map/gather_and_match/pallas_call | solution.py:420
  27.2 47.2 %finish.1 = f32[24,128]{1,0:T(8,128)} custom-call(s32[256]{0:T(256)} %cnt_in.3, f32[32,128]{1,0:T(8,128)} %get-tuple-element.7.fast_ref, bf16[1,64,1024]{2,1,0:T(8,128)(2,1)} %feat_ref.1, bf16[1,3,1024]{2,1,0:T(4,128)(2,1)} %pos_ref.1, bf16[12,544,128]{2,1,0:T(8,128)(2,1)} %get-tuple-element.8.kept_ref), custom_call_target="tpu_custom_call" | custom-call | tf_op jit(solution)/shard_map/finish/pallas_call | solution.py:451

commit v6 on v5

--- a/solution.py
+++ b/solution.py
@@ -31,20 +31,20 @@
 XM = SLOTS
 ORDERS = (
     (0, 1, 2, 3, 4, 5, 6, 7, 8, 9, 10, 11),
-    (0, 1, 4, 6, 7, 10, 2, 3, 8, 5, 9, 11),
+    (0, 1, 4, 6, 2, 7, 3, 10, 8, 5, 9, 11),
     (0, 2, 3, 6, 5, 8, 1, 9, 4, 7, 10, 11),
     (0, 1, 2, 3, 4, 6, 7, 8, 9, 10, 5, 11),
-    (0, 2, 3, 6, 5, 8, 9, 1, 7, 4, 11, 10),
+    (0, 2, 3, 6, 5, 9, 8, 1, 4, 7, 11, 10),
     (0, 1, 4, 6, 7, 2, 10, 3, 8, 5, 9, 11),
     (0, 2, 3, 5, 8, 6, 9, 11, 1, 4, 7, 10),
 )
 KINDS = (1, 2, 3, 0, 0, 0, 0, 0, 0, 0, 0, 0, 0, 3, 4, 5)
 RELAY_STEPS = {
     1: (1, 1, 5, 1, 7, 1, 8),
-    2: (2, 6, 1, 2, 1, 5, 1),
+    2: (2, 4, 1, 2, 1, 5, 1),
     XM: (3, 3, 3, 3, 3, 3, 3),
-    7: (7, 4, 8, 6, 8, 4, 10),
-    8: (7, 8, 5, 7, 5, 8, 4),
+    7: (7, 5, 9, 6, 9, 4, 10),
+    8: (7, 8, 5, 7, 6, 8, 4),
 }
 BACK_STEP = 3
 CROSS_STEP = 1

time: 74.9 us -> 74.6 us (level)
  the two profiles are of different devices: /device:TPU:251 before, /device:TPU:243 now
where the time goes in v6:
time: 74.6 us; the launch traced here: 74.1 us
  Pallas kernels  74.1 us (99%)
    pallas_call x1, Pallas kernels, per_device(): pl.pallas_call(functools.partial(finish, total), out_shape=jax.ShapeDtype...  47.2 us
    pallas_call x1, Pallas kernels, per_device(): pl.pallas_call(functools.partial(gather_and_match, total), out_shape=[jax...  26.9 us

profile of v6, /device:TPU:243, one launch (start us, length us, event | category | flops | bytes accessed | tf_op | source)
XLA Modules:
  0.0 74.1 jit_solution(18286709413918367482)
XLA Ops:
  0.0 26.9 %gather_and_match.1 = (f32[32,128]{1,0:T(8,128)}, bf16[12,544,128]{2,1,0:T(8,128)(2,1)}) custom-call(s32[256]{0:T(256)} %cnt_in.3, bf16[1,64,1024]{2,1,0:T(8,128)(2,1)} %feat_ref.1, bf16[1,3,1024]{2,1,0:T(4,128)(2,1)} %pos_ref.1), custom_call_target="tpu_custom_call" | custom-call | tf_op jit(solution)/shard_map/gather_and_match/pallas_call | solution.py:420
  26.9 47.2 %finish.1 = f32[24,128]{1,0:T(8,128)} custom-call(s32[256]{0:T(256)} %cnt_in.3, f32[32,128]{1,0:T(8,128)} %get-tuple-element.7.fast_ref, bf16[1,64,1024]{2,1,0:T(8,128)(2,1)} %feat_ref.1, bf16[1,3,1024]{2,1,0:T(4,128)(2,1)} %pos_ref.1, bf16[12,544,128]{2,1,0:T(8,128)(2,1)} %get-tuple-element.8.kept_ref), custom_call_target="tpu_custom_call" | custom-call | tf_op jit(solution)/shard_map/finish/pallas_call | solution.py:451
